TPU v7x, 32 devices: a whole 2x2x4 slice. The times are simulated.
32 devices in a mesh: gx: 4 (over z), gy: 4 (over y, core), gz: 2 (over x).
Axes of the slice: x: 2, y: 2, z: 4, core: 2. Of those that a mesh axis runs over, the one named last changes fastest.
Arguments:
- tokens: bfloat16 [32, 32, 16, 384], P('gx', 'gy', 'gz'), may hold values from -60 to 60
- frozen: int32 [32, 32, 16], P('gx', 'gy', 'gz'), may hold values 0 or 1
- cotangent: bfloat16 [32, 32, 16, 384], P('gx', 'gy', 'gz'), may hold values from -6 to 6
- w_qkv: bfloat16 [384, 1152], replicated, may hold values from -0.3125 to 0.3125
- w_proj: bfloat16 [384, 384], replicated, may hold values from -0.3125 to 0.3125
- norm_gain: float32 [384], replicated, may hold values from 0.5 to 8
Outputs:
- block_out: bfloat16 [32, 32, 16, 384], P('gx', 'gy', 'gz')
- tokens_grad: bfloat16 [32, 32, 16, 384], P('gx', 'gy', 'gz')
- qkv_grad: float32 [384, 1152], replicated
- proj_grad: float32 [384, 384], replicated
- gain_grad: float32 [384], replicated
All inputs are finite; a program needn't handle non-finite values. No bound on the sum of `frozen` on one device may be relied on, other than what follows from the above.
Results may differ from a plain program's by a relative error of at most 0.015.
The roundings to bfloat16 on the way count: a program that leaves them out, or rounds other values in their place, can miss the bound.
Values may be sent and summed in bfloat16 or wider, within the bound.
A program may use at most 64 MiB of HBM per device.

v0:
```python
import jax
import jax.numpy as jnp
from jax import lax
from jax.sharding import PartitionSpec as P

D = 384
HEADS = 12
HDIM = 32
WIN = 8


EPSILON = 1e-05


def shifted_2(block, axis, distance):
    devices = range(lax.axis_size(axis))
    route = [((i - distance) % len(devices), i) for i in devices]
    return lax.ppermute(block, axis, route)


def group_pass(queries, key_rows, values, d_mixed):
    score_scale = HDIM ** (-0.5)
    scores = (
        jnp.einsum("qhd,khd->hqk", queries, key_rows, preferred_element_type=jnp.float32)
        * score_scale
    )
    top_score = jnp.max(scores, axis=-1, keepdims=True)
    exp_terms = jnp.exp(scores - top_score)
    attn_probs = exp_terms / jnp.sum(exp_terms, axis=-1, keepdims=True)
    probs_low = attn_probs.astype(jnp.bfloat16)
    mixed_group = jnp.einsum(
        "hqk,khd->qhd", probs_low, values, preferred_element_type=jnp.float32
    ).astype(jnp.bfloat16)
    d_values = jnp.einsum(
        "hqk,qhd->khd", probs_low, d_mixed, preferred_element_type=jnp.float32
    ).astype(jnp.bfloat16)
    d_probs = jnp.einsum("qhd,khd->hqk", d_mixed, values, preferred_element_type=jnp.float32)
    d_scores = (
        attn_probs * (d_probs - jnp.sum(attn_probs * d_probs, axis=-1, keepdims=True)) * score_scale
    ).astype(jnp.bfloat16)
    d_queries = jnp.einsum(
        "hqk,khd->qhd", d_scores, key_rows, preferred_element_type=jnp.float32
    ).astype(jnp.bfloat16)
    d_keys = jnp.einsum(
        "hqk,qhd->khd", d_scores, queries, preferred_element_type=jnp.float32
    ).astype(jnp.bfloat16)
    return (mixed_group, d_queries, d_keys, d_values)


def window_pass(window_rows, window_cot, w_qkv, w_proj, norm_gain):
    row_count = window_rows.shape[0]
    groups = 2
    per_group = HEADS // groups
    widened = window_rows.astype(jnp.float32)
    row_mean = jnp.mean(widened, axis=-1, keepdims=True)
    centred = widened - row_mean
    inv_std = lax.rsqrt(jnp.mean(centred * centred, axis=-1, keepdims=True) + EPSILON)
    unit_rows = centred * inv_std
    normed = (unit_rows * norm_gain).astype(jnp.bfloat16)
    qkv_rows = jnp.dot(normed, w_qkv, preferred_element_type=jnp.float32).astype(jnp.bfloat16)
    d_mixed = jnp.dot(window_cot, w_proj.T, preferred_element_type=jnp.float32).astype(jnp.bfloat16)

    def grouped(rows):
        return rows.reshape(row_count, groups, per_group, HDIM).transpose(1, 0, 2, 3)

    def ungrouped(parts):
        return parts.transpose(1, 0, 2, 3).reshape(row_count, D)

    outputs = lax.map(
        lambda packed: group_pass(*packed),
        (
            grouped(qkv_rows[:, :D]),
            grouped(qkv_rows[:, D : 2 * D]),
            grouped(qkv_rows[:, 2 * D :]),
            grouped(d_mixed),
        ),
    )
    mixed_rows = ungrouped(outputs[0])
    branch = jnp.dot(mixed_rows, w_proj, preferred_element_type=jnp.float32).astype(jnp.bfloat16)
    d_qkv = jnp.concatenate(
        [ungrouped(outputs[1]), ungrouped(outputs[2]), ungrouped(outputs[3])], axis=1
    )
    proj_term = jnp.dot(mixed_rows.T, window_cot, preferred_element_type=jnp.float32)
    qkv_term = jnp.dot(normed.T, d_qkv, preferred_element_type=jnp.float32)
    d_normed = jnp.dot(d_qkv, w_qkv.T, preferred_element_type=jnp.float32)
    gain_term = jnp.sum(d_normed * unit_rows, axis=0)
    scaled_grad = d_normed * norm_gain
    d_rows = (
        inv_std
        * (
            scaled_grad
            - jnp.mean(scaled_grad, axis=-1, keepdims=True)
            - unit_rows * jnp.mean(scaled_grad * unit_rows, axis=-1, keepdims=True)
        )
    ).astype(jnp.bfloat16)
    return (branch, d_rows, qkv_term, proj_term, gain_term)


def partition(block):
    first, second, third, width = block.shape
    grid = block.reshape(first // WIN, WIN, second // WIN, WIN, third // WIN, WIN, width)
    return grid.transpose(0, 2, 4, 1, 3, 5, 6).reshape(-1, WIN**3, width)


def assemble(windows, first, second, third):
    grid = windows.reshape(
        first // WIN, second // WIN, third // WIN, WIN, WIN, WIN, windows.shape[-1]
    )
    return grid.transpose(0, 3, 1, 4, 2, 5, 6).reshape(first, second, third, windows.shape[-1])


def border(stacked, axis_pos, direction):
    half_width = WIN // 2
    extent = stacked.shape[axis_pos]
    if direction < 0:
        return lax.slice_in_dim(stacked, 0, half_width, axis=axis_pos)
    return lax.slice_in_dim(stacked, extent - half_width, extent, axis=axis_pos)


def attach(stacked, arrived, axis_pos, direction):
    half_width = WIN // 2
    extent = stacked.shape[axis_pos]
    if direction < 0:
        return jnp.concatenate(
            [lax.slice_in_dim(stacked, half_width, extent, axis=axis_pos), arrived], axis=axis_pos
        )
    return jnp.concatenate(
        [arrived, lax.slice_in_dim(stacked, 0, extent - half_width, axis=axis_pos)], axis=axis_pos
    )


def roll_half(stacked, direction):
    stacked = attach(
        stacked, shifted_2(border(stacked, 1, direction), "gx", direction), 1, direction
    )
    stacked = attach(
        stacked, shifted_2(border(stacked, 2, direction), "gy", direction), 2, direction
    )
    stacked = attach(
        stacked, shifted_2(border(stacked, 3, direction), "gz", direction), 3, direction
    )
    return stacked


def local(tokens, frozen, cotangent, w_qkv, w_proj, norm_gain):
    kept = jnp.where(frozen[..., None] == 1, tokens, jnp.zeros_like(tokens))
    shifted = roll_half(jnp.stack([kept, cotangent]), -1)
    zeros_init = (
        jnp.zeros((D, 3 * D), jnp.float32),
        jnp.zeros((D, D), jnp.float32),
        jnp.zeros((D,), jnp.float32),
    )

    def window_step(totals, window_pair):
        results = window_pass(window_pair[0], window_pair[1], w_qkv, w_proj, norm_gain)
        return (
            (totals[0] + results[2], totals[1] + results[3], totals[2] + results[4]),
            (results[0], results[1]),
        )

    totals, blocks = lax.scan(
        window_step, zeros_init, (partition(shifted[0]), partition(shifted[1]))
    )
    first, second, third = (tokens.shape[0], tokens.shape[1], tokens.shape[2])
    returned = jnp.stack(
        [assemble(blocks[0], first, second, third), assemble(blocks[1], first, second, third)]
    )
    restored = roll_half(returned, 1)
    summed = lax.psum((totals[0], totals[1], totals[2]), ("gx", "gy", "gz"))
    block_out = (kept.astype(jnp.float32) + restored[0].astype(jnp.float32)).astype(jnp.bfloat16)
    tokens_grad = jnp.where(
        frozen[..., None] == 1,
        cotangent.astype(jnp.float32) + restored[1].astype(jnp.float32),
        jnp.zeros((), jnp.float32),
    ).astype(jnp.bfloat16)
    everyone = (
        first * second * third * lax.axis_size("gx") * lax.axis_size("gy") * lax.axis_size("gz")
    )
    grad_scale = everyone ** (-0.5)
    return (
        block_out,
        tokens_grad,
        summed[0] * grad_scale,
        summed[1] * grad_scale,
        summed[2] * grad_scale,
    )


def solution(mesh):
    placed = (
        P("gx", "gy", "gz", None),
        P("gx", "gy", "gz"),
        P("gx", "gy", "gz", None),
        P(),
        P(),
        P(),
    )
    return jax.shard_map(
        local,
        mesh=mesh,
        in_specs=placed,
        out_specs=(P("gx", "gy", "gz", None), P("gx", "gy", "gz", None), P(), P(), P()),
        check_vma=False,
    )
```

profile of v0, /device:TPU:1, one launch (start us, length us, event | category | flops | bytes accessed | tf_op | source)
XLA Modules:
  0.0 281.8 jit_solution(15544111670739164715)
XLA Ops:
  10.3 4.2 %collective-permute-start = (bf16[2,4,8,8,384]{4,3,2,1,0:T(8,128)(2,1)S(1)}, bf16[2,4,8,8,384]{4,3,2,1,0:T(8,128)(2,1)S(1)}, u32[]{:S(2)}, u32[]{:S(2)}) collective-permute-start(bf16[2,4,8,8,384]{4,3,2,1,0:T(8,128)(2,1)S(1)} %get-tuple-element.131), channel_id=1, source_target_pairs={{8,0},{16,8},{24,16},{0,24},{9,1},{17,9},{25,17},{1,25},{10,2},{18... | collective-permute-start | bytes 1179656 | tf_op jit(solution)/shard_map/ppermute | solution.py:18
  14.6 7.8 %collective-permute-done = bf16[2,4,8,8,384]{4,3,2,1,0:T(8,128)(2,1)S(1)} collective-permute-done((bf16[2,4,8,8,384]{4,3,2,1,0:T(8,128)(2,1)S(1)}, bf16[2,4,8,8,384]{4,3,2,1,0:T(8,128)(2,1)S(1)}, u32[]{:S(2)}, u32[]{:S(2)}) %collective-permute-start) | collective-permute-done | bytes 393248 | tf_op jit(solution)/shard_map/ppermute | solution.py:18
  24.0 6.6 %collective-permute-done.1 = bf16[2,8,4,8,384]{4,3,2,1,0:T(8,128)(2,1)S(1)} collective-permute-done((bf16[2,8,4,8,384]{4,3,2,1,0:T(8,128)(2,1)S(1)}, bf16[2,8,4,8,384]{4,3,2,1,0:T(8,128)(2,1)S(1)}, u32[]{:S(2)}, u32[]{:S(2)}) %collective-permute-start.1) | collective-permute-done | bytes 393248 | tf_op jit(solution)/shard_map/ppermute | solution.py:18
  32.2 8.9 %collective-permute-done.2 = bf16[2,8,8,4,384]{4,3,2,1,0:T(4,128)(2,1)S(1)} collective-permute-done((bf16[2,8,8,4,384]{4,3,2,1,0:T(4,128)(2,1)S(1)}, bf16[2,8,8,4,384]{4,3,2,1,0:T(4,128)(2,1)S(1)}, u32[]{:S(2)}, u32[]{:S(2)}) %collective-permute-start.2) | collective-permute-done | bytes 393248 | tf_op jit(solution)/shard_map/ppermute | solution.py:18
  46.4 76.5 %while.30 = (s32[]{:T(128)}, bf16[2,512,6,32]{1,3,2,0:T(8,128)(2,1)}, bf16[2,512,6,32]{1,3,2,0:T(8,128)(2,1)}, bf16[2,512,6,32]{1,3,2,0:T(8,128)(2,1)}, bf16[2,5...) while((s32[]{:T(128)}, ...), condition=%wide.region_6.7_spmd, body=%wide.region_2.6_spmd.sunk | while | flops 637410816 | bytes 84265168 | solution.py:69
  46.6 4.8 %fusion.173 = (f32[6,512]{1,0:T(8,128)S(1)}, f32[6,512,512]{1,2,0:T(8,128)}) fusion(bf16[2,512,6,32]{1,3,2,0:T(8,128)(2,1)S(1)} %get-tuple-element.221, s32[]{:T(128)} %get-tuple-element.204, bf16[2,512,6,32]{1,3,2,0:T(8,128)(2,1)S(1)} %get-tuple-element.220), kind=kOutput, calls=%fused_computation.123.clone.1 | convolution fusion | flops 105382400 | bytes 6697984 | tf_op jit(solution)/shard_map/while/body/eval_jaxpr/while/body/eval_jaxpr/sub | solution.py:28
  51.4 3.7 %fusion.175 = f32[6,512,512]{1,2,0:T(8,128)} fusion(bf16[2,512,6,32]{1,3,2,0:T(8,128)(2,1)S(1)} %get-tuple-element.222, s32[]{:T(128)} %get-tuple-element.204, bf16[2,512,6,32]{1,3,2,0:T(8,128)(2,1)S(1)} %get-tuple-element.219), kind=kOutput, calls=%fused_computation.30.clone.1 | convolution fusion | flops 100663296 | bytes 6685696 | tf_op jit(solution)/shard_map/while/body/eval_jaxpr/while/body/eval_jaxpr/qhd,khd->hqk/dot_general | solution.py:37
  55.0 9.3 %fusion.177 = bf16[2,512,6,32]{1,3,2,0:T(8,128)(2,1)S(1)} fusion(bf16[2,512,6,32]{1,3,2,0:T(8,128)(2,1)S(1)} %copy-done.23, s32[]{:T(128)} %get-tuple-element.204, f32[6,512,512]{1,2,0:T(8,128)} %fusion.175, bf16[2,512,6,32]{1,3,2,0:T(8,128)(2,1)S(1)} %get-tuple-element.220, f32[6,512,512]{1,2,0:T(8,128)} %get-tuple-element.192, ...), kind=kOutput, calls=%fused_computation.25.clone.1 | convolution fusion | flops 111775232 | bytes 25592832 | tf_op jit(solution)/shard_map/while/body/eval_jaxpr/while/body/eval_jaxpr/hqk,qhd->khd/dot_general | solution.py:44
  64.3 11.6 %fusion.176 = bf16[2,512,6,32]{1,3,2,0:T(8,128)(2,1)} fusion(bf16[2,512,6,32]{1,3,2,0:T(8,128)(2,1)} %get-tuple-element.206, s32[]{:T(128)} %get-tuple-element.204, f32[6,512,512]{1,2,0:T(8,128)} %fusion.175, bf16[2,512,6,32]{1,3,2,0:T(8,128)(2,1)S(1)} %get-tuple-element.221, f32[6,512,512]{1,2,0:T(8,128)} %get-tuple-element.192, ...), kind=kOutput, calls=%fused_computation.27.clone.1 | convolution fusion | flops 111775232 | bytes 25592832 | tf_op jit(solution)/shard_map/while/body/eval_jaxpr/while/body/eval_jaxpr/hqk,khd->qhd/dot_general | solution.py:41
  75.9 4.6 %fusion.178 = bf16[2,512,6,32]{1,3,2,0:T(8,128)(2,1)} fusion(bf16[2,512,6,32]{1,3,2,0:T(8,128)(2,1)} %get-tuple-element.208, s32[]{:T(128)} %get-tuple-element.204, bf16[2,512,6,32]{1,3,2,0:T(8,128)(2,1)S(1)} %get-tuple-element.222, f32[6,512,512]{1,2,0:T(8,128)} %get-tuple-element.192, f32[6,512]{1,0:T(8,128)S(1)} %get-tuple-element.193), kind=kOutput, calls=%fused_computation.21.clone.1 | convolution fusion | flops 103907328 | bytes 6702080 | tf_op jit(solution)/shard_map/while/body/eval_jaxpr/while/body/eval_jaxpr/hqk,qhd->khd/dot_general | solution.py:34
  80.5 3.4 %fusion.174 = bf16[2,512,6,32]{1,3,2,0:T(8,128)(2,1)S(1)} fusion(bf16[2,512,6,32]{1,3,2,0:T(8,128)(2,1)S(1)} %copy-done.9, s32[]{:T(128)} %get-tuple-element.204, bf16[2,512,6,32]{1,3,2,0:T(8,128)(2,1)S(1)} %get-tuple-element.219, f32[6,512,512]{1,2,0:T(8,128)} %get-tuple-element.192, f32[6,512]{1,0:T(8,128)S(1)} %get-tuple-element.193), kind=kOutput, calls=%fused_computation.23.clone.1 | convolution fusion | flops 103907328 | bytes 6702080 | tf_op jit(solution)/shard_map/while/body/eval_jaxpr/while/body/eval_jaxpr/hqk,khd->qhd/dot_general | solution.py:31
  84.7 4.8 %fusion.173 = (f32[6,512]{1,0:T(8,128)S(1)}, f32[6,512,512]{1,2,0:T(8,128)}) fusion(bf16[2,512,6,32]{1,3,2,0:T(8,128)(2,1)S(1)} %get-tuple-element.221, s32[]{:T(128)} %get-tuple-element.204, bf16[2,512,6,32]{1,3,2,0:T(8,128)(2,1)S(1)} %get-tuple-element.220), kind=kOutput, calls=%fused_computation.123.clone.1 | convolution fusion | flops 105382400 | bytes 6697984 | tf_op jit(solution)/shard_map/while/body/eval_jaxpr/while/body/eval_jaxpr/sub | solution.py:28
  89.5 3.7 %fusion.175 = f32[6,512,512]{1,2,0:T(8,128)} fusion(bf16[2,512,6,32]{1,3,2,0:T(8,128)(2,1)S(1)} %get-tuple-element.222, s32[]{:T(128)} %get-tuple-element.204, bf16[2,512,6,32]{1,3,2,0:T(8,128)(2,1)S(1)} %get-tuple-element.219), kind=kOutput, calls=%fused_computation.30.clone.1 | convolution fusion | flops 100663296 | bytes 6685696 | tf_op jit(solution)/shard_map/while/body/eval_jaxpr/while/body/eval_jaxpr/qhd,khd->hqk/dot_general | solution.py:37
  93.2 9.3 %fusion.177 = bf16[2,512,6,32]{1,3,2,0:T(8,128)(2,1)S(1)} fusion(bf16[2,512,6,32]{1,3,2,0:T(8,128)(2,1)S(1)} %copy-done.23, s32[]{:T(128)} %get-tuple-element.204, f32[6,512,512]{1,2,0:T(8,128)} %fusion.175, bf16[2,512,6,32]{1,3,2,0:T(8,128)(2,1)S(1)} %get-tuple-element.220, f32[6,512,512]{1,2,0:T(8,128)} %get-tuple-element.192, ...), kind=kOutput, calls=%fused_computation.25.clone.1 | convolution fusion | flops 111775232 | bytes 25592832 | tf_op jit(solution)/shard_map/while/body/eval_jaxpr/while/body/eval_jaxpr/hqk,qhd->khd/dot_general | solution.py:44
  102.4 11.6 %fusion.176 = bf16[2,512,6,32]{1,3,2,0:T(8,128)(2,1)} fusion(bf16[2,512,6,32]{1,3,2,0:T(8,128)(2,1)} %get-tuple-element.206, s32[]{:T(128)} %get-tuple-element.204, f32[6,512,512]{1,2,0:T(8,128)} %fusion.175, bf16[2,512,6,32]{1,3,2,0:T(8,128)(2,1)S(1)} %get-tuple-element.221, f32[6,512,512]{1,2,0:T(8,128)} %get-tuple-element.192, ...), kind=kOutput, calls=%fused_computation.27.clone.1 | convolution fusion | flops 111775232 | bytes 25592832 | tf_op jit(solution)/shard_map/while/body/eval_jaxpr/while/body/eval_jaxpr/hqk,khd->qhd/dot_general | solution.py:41
  114.1 4.6 %fusion.178 = bf16[2,512,6,32]{1,3,2,0:T(8,128)(2,1)} fusion(bf16[2,512,6,32]{1,3,2,0:T(8,128)(2,1)} %get-tuple-element.208, s32[]{:T(128)} %get-tuple-element.204, bf16[2,512,6,32]{1,3,2,0:T(8,128)(2,1)S(1)} %get-tuple-element.222, f32[6,512,512]{1,2,0:T(8,128)} %get-tuple-element.192, f32[6,512]{1,0:T(8,128)S(1)} %get-tuple-element.193), kind=kOutput, calls=%fused_computation.21.clone.1 | convolution fusion | flops 103907328 | bytes 6702080 | tf_op jit(solution)/shard_map/while/body/eval_jaxpr/while/body/eval_jaxpr/hqk,qhd->khd/dot_general | solution.py:34
  118.6 3.4 %fusion.174 = bf16[2,512,6,32]{1,3,2,0:T(8,128)(2,1)S(1)} fusion(bf16[2,512,6,32]{1,3,2,0:T(8,128)(2,1)S(1)} %copy-done.9, s32[]{:T(128)} %get-tuple-element.204, bf16[2,512,6,32]{1,3,2,0:T(8,128)(2,1)S(1)} %get-tuple-element.219, f32[6,512,512]{1,2,0:T(8,128)} %get-tuple-element.192, f32[6,512]{1,0:T(8,128)S(1)} %get-tuple-element.193), kind=kOutput, calls=%fused_computation.23.clone.1 | convolution fusion | flops 103907328 | bytes 6702080 | tf_op jit(solution)/shard_map/while/body/eval_jaxpr/while/body/eval_jaxpr/hqk,khd->qhd/dot_general | solution.py:31
  122.9 3.2 %fusion.109 = f32[384,1152]{1,0:T(8,128)} fusion(bf16[512,384]{1,0:T(8,128)(2,1)S(1)} %copy-done.8, bf16[512,384]{0,1:T(8,128)(2,1)} %bitcast.163, bf16[512,384]{0,1:T(8,128)(2,1)} %bitcast.161, bf16[512,384]{0,1:T(8,128)(2,1)} %bitcast.28), kind=kOutput, calls=%fused_computation.98 | convolution fusion | flops 456523776 | bytes 3342336 | tf_op jit(solution)/shard_map/while/body/eval_jaxpr/dot_general | solution.py:84
  126.1 2.5 multiply_reduce_fusion.2
  131.0 12.2 %collective-permute-done.3 = bf16[2,4,8,8,384]{4,3,2,1,0:T(8,128)(2,1)S(1)} collective-permute-done((bf16[2,4,8,8,384]{4,3,2,1,0:T(8,128)(2,1)S(1)}, bf16[2,4,8,8,384]{4,3,2,1,0:T(8,128)(2,1)S(1)}, u32[]{:S(2)}, u32[]{:S(2)}) %collective-permute-start.3) | collective-permute-done | bytes 393248 | tf_op jit(solution)/shard_map/ppermute | solution.py:18
  143.4 2.3 collective-permute-start.4
  145.7 37.9 %psum.23 = f32[384]{0:T(512)S(1)} all-reduce(f32[384]{0:T(512)S(1)} %get-tuple-element.92), channel_id=1, replica_groups=mesh['gx'=4,'gy'=4,'gz'=2] {'gx','gy','gz'}, use_global_device_ids=true, to_apply=%region_12.13 | all-reduce | flops 384 | bytes 3072 | tf_op jit(solution)/shard_map/psum | solution.py:169
  186.3 82.3 %all-reduce.3.cloned.1.call-done = (f32[384,1152]{1,0:T(8,128)}, f32[384,384]{1,0:T(8,128)}) async-done(((f32[384,1152]{1,0:T(8,128)}, f32[384,384]{1,0:T(8,128)}), (f32[384,1152]{1,0:T(8,128)}, f32[384,384]{1,0:T(8,128)})) %all-reduce.3.cloned.1.call-update) | async-done | bytes 2359312 | tf_op jit(solution)/shard_map/psum | solution.py:169
  268.6 2.8 broadcast_multiply_fusion
  (101 shorter events, 21.7 us)
Async XLA Ops:
  7.2 35.3 %copy-start = (bf16[384,1152]{1,0:T(8,128)(2,1)S(1)}, bf16[384,1152]{1,0:T(8,128)(2,1)}, u32[]{:S(2)}) copy-start(bf16[384,1152]{1,0:T(8,128)(2,1)} %param.11) | copy-start | bytes 2654212
  7.2 34.7 %copy-start.21 = (f32[384]{0:T(512)S(1)}, f32[384]{0:T(512)}, u32[]{:S(2)}) copy-start(f32[384]{0:T(512)} %param.13) | copy-start | bytes 4612
  7.2 261.4 %all-reduce.3.cloned.1.call-start = ((), (), s32[]{:S(2)}) async-start(), calls=%async_computation | async-start | bytes 4718592 | tf_op jit(solution)/shard_map/psum | solution.py:169
  10.3 12.0 %collective-permute-start = (bf16[2,4,8,8,384]{4,3,2,1,0:T(8,128)(2,1)S(1)}, bf16[2,4,8,8,384]{4,3,2,1,0:T(8,128)(2,1)S(1)}, u32[]{:S(2)}, u32[]{:S(2)}) collective-permute-start(bf16[2,4,8,8,384]{4,3,2,1,0:T(8,128)(2,1)S(1)} %get-tuple-element.131), channel_id=1, source_target_pairs={{8,0},{16,8},{24,16},{0,24},{9,1},{17,9},{25,17},{1,25},{10,2},{18... | collective-permute-start | bytes 1179656 | tf_op jit(solution)/shard_map/ppermute | solution.py:18
  22.4 8.2 %collective-permute-start.1 = (bf16[2,8,4,8,384]{4,3,2,1,0:T(8,128)(2,1)S(1)}, bf16[2,8,4,8,384]{4,3,2,1,0:T(8,128)(2,1)S(1)}, u32[]{:S(2)}, u32[]{:S(2)}) collective-permute-start(bf16[2,8,4,8,384]{4,3,2,1,0:T(8,128)(2,1)S(1)} %get-tuple-element.129), channel_id=1, source_target_pairs={{2,0},{4,2},{6,4},{0,6},{3,1},{5,3},{7,5},{1,7},{10,8},{12,10},{14... | collective-permute-start | bytes 1179656 | tf_op jit(solution)/shard_map/ppermute | solution.py:18
  30.6 15.3 %copy-start.13 = (bf16[384,384]{1,0:T(8,128)(2,1)S(1)}, bf16[384,384]{1,0:T(8,128)(2,1)}, u32[]{:S(2)}) copy-start(bf16[384,384]{1,0:T(8,128)(2,1)} %param.12) | copy-start | bytes 884740
  30.9 10.2 %collective-permute-start.2 = (bf16[2,8,8,4,384]{4,3,2,1,0:T(4,128)(2,1)S(1)}, bf16[2,8,8,4,384]{4,3,2,1,0:T(4,128)(2,1)S(1)}, u32[]{:S(2)}, u32[]{:S(2)}) collective-permute-start(bf16[2,8,8,4,384]{4,3,2,1,0:T(4,128)(2,1)S(1)} %get-tuple-element.127), channel_id=1, source_target_pairs={{1,0},{0,1},{3,2},{2,3},{5,4},{4,5},{7,6},{6,7},{9,8},{8,9},{11,10... | collective-permute-start | bytes 1179656 | tf_op jit(solution)/shard_map/ppermute | solution.py:18
  41.3 5.0 %copy-start.1 = (bf16[1,8,8,8,384]{4,3,2,1,0:T(8,128)(2,1)}, bf16[1,8,8,8,384]{4,3,2,1,0:T(8,128)(2,1)S(1)}, u32[]{:S(2)}) copy-start(bf16[1,8,8,8,384]{4,3,2,1,0:T(8,128)(2,1)S(1)} %get-tuple-element.116) | copy-start | bytes 1179652
  46.3 76.5 %copy-start.8 = (bf16[512,384]{1,0:T(8,128)(2,1)S(1)}, bf16[512,384]{1,0:T(8,128)(2,1)}, u32[]{:S(2)}) copy-start(bf16[512,384]{1,0:T(8,128)(2,1)} %copy-done.7) | copy-start | bytes 1179652
  46.3 79.8 %copy-start.18 = (f32[512]{0:T(512)S(1)}, f32[512]{0:T(512)}, u32[]{:S(2)}) copy-start(f32[512]{0:T(512)} %copy-done.17) | copy-start | bytes 6148
  46.3 79.8 %copy-start.20 = (f32[512]{0:T(512)S(1)}, f32[512]{0:T(512)}, u32[]{:S(2)}) copy-start(f32[512]{0:T(512)} %copy-done.19) | copy-start | bytes 6148
  46.4 79.8 %copy-start.22 = (f32[384]{0:T(512)S(1)}, f32[384]{0:T(512)}, u32[]{:S(2)}) copy-start(f32[384]{0:T(512)} %param.13) | copy-start | bytes 4612
  64.3 11.6 %copy-start.24 = (bf16[2,512,6,32]{1,3,2,0:T(8,128)(2,1)}, bf16[2,512,6,32]{1,3,2,0:T(8,128)(2,1)S(1)}, u32[]{:S(2)}) copy-start(bf16[2,512,6,32]{1,3,2,0:T(8,128)(2,1)S(1)} %fusion.177) | copy-start | bytes 1179652 | tf_op jit(solution)/shard_map/while/body/eval_jaxpr/while
  102.4 11.6 %copy-start.24 = (bf16[2,512,6,32]{1,3,2,0:T(8,128)(2,1)}, bf16[2,512,6,32]{1,3,2,0:T(8,128)(2,1)S(1)}, u32[]{:S(2)}) copy-start(bf16[2,512,6,32]{1,3,2,0:T(8,128)(2,1)S(1)} %fusion.177) | copy-start | bytes 1179652 | tf_op jit(solution)/shard_map/while/body/eval_jaxpr/while
  114.1 4.6 %copy-start.9 = (bf16[2,512,6,32]{1,3,2,0:T(8,128)(2,1)S(1)}, bf16[2,512,6,32]{1,3,2,0:T(8,128)(2,1)}, u32[]{:S(2)}) copy-start(bf16[2,512,6,32]{1,3,2,0:T(8,128)(2,1)} %get-tuple-element.205) | copy-start | bytes 1179652 | tf_op jit(solution)/shard_map/while/body/eval_jaxpr/while
  122.8 5.8 %copy-start.11 = (bf16[2,512,6,32]{1,3,2,0:T(8,128)(2,1)S(1)}, bf16[2,512,6,32]{1,3,2,0:T(8,128)(2,1)}, u32[]{:S(2)}) copy-start(bf16[2,512,6,32]{1,3,2,0:T(8,128)(2,1)} %get-tuple-element.88) | copy-start | bytes 1179652
  122.8 5.8 %copy-start.14 = (bf16[384,384]{1,0:T(8,128)(2,1)S(1)}, bf16[384,384]{1,0:T(8,128)(2,1)}, u32[]{:S(2)}) copy-start(bf16[384,384]{1,0:T(8,128)(2,1)} %param.12) | copy-start | bytes 884740
  122.8 6.3 %copy-start.2 = (bf16[1,8,8,8,384]{4,3,2,1,0:T(8,128)(2,1)S(1)}, bf16[1,8,8,8,384]{4,3,2,1,0:T(8,128)(2,1)}, u32[]{:S(2)}) copy-start(bf16[1,8,8,8,384]{4,3,2,1,0:T(8,128)(2,1)} %copy-done.1) | copy-start | bytes 1179652
  129.6 13.6 %collective-permute-start.3 = (bf16[2,4,8,8,384]{4,3,2,1,0:T(8,128)(2,1)S(1)}, bf16[2,4,8,8,384]{4,3,2,1,0:T(8,128)(2,1)S(1)}, u32[]{:S(2)}, u32[]{:S(2)}) collective-permute-start(bf16[2,4,8,8,384]{4,3,2,1,0:T(8,128)(2,1)S(1)} %fusion.112), channel_id=1, source_target_pairs={{24,0},{0,8},{8,16},{16,24},{25,1},{1,9},{9,17},{17,25},{26,2},{2,... | collective-permute-start | bytes 1179656 | tf_op jit(solution)/shard_map/ppermute | solution.py:18
  131.0 142.7 %copy-start.5 = (bf16[8,8,8,384]{3,2,1,0:T(8,128)(2,1)S(1)}, bf16[8,8,8,384]{3,2,1,0:T(8,128)(2,1)}, u32[]{:S(2)}) copy-start(bf16[8,8,8,384]{3,2,1,0:T(8,128)(2,1)} %param.10) | copy-start | bytes 1179652
  131.0 142.7 %copy-start.6 = (bf16[8,8,8,384]{3,2,1,0:T(8,128)(2,1)S(1)}, bf16[8,8,8,384]{3,2,1,0:T(8,128)(2,1)}, u32[]{:S(2)}) copy-start(bf16[8,8,8,384]{3,2,1,0:T(8,128)(2,1)} %param.8) | copy-start | bytes 1179652
  131.0 142.7 %copy-start.16 = (pred[8,8,8]{2,1,0:T(8,128)(4,1)S(1)}, pred[8,8,8]{2,1,0:T(8,128)(4,1)}, u32[]{:S(2)}) copy-start(pred[8,8,8]{2,1,0:T(8,128)(4,1)} %copy-done.15) | copy-start | bytes 1540
  143.4 40.8 %collective-permute-start.4 = (bf16[2,8,4,8,384]{4,3,2,1,0:T(8,128)(2,1)S(1)}, bf16[2,8,4,8,384]{4,3,2,1,0:T(8,128)(2,1)S(1)}, u32[]{:S(2)}, u32[]{:S(2)}) collective-permute-start(bf16[2,8,4,8,384]{4,3,2,1,0:T(8,128)(2,1)S(1)} %get-tuple-element.124), channel_id=1, source_target_pairs={{6,0},{0,2},{2,4},{4,6},{7,1},{1,3},{3,5},{5,7},{14,8},{8,10},{10,... | collective-permute-start | bytes 1179656 | tf_op jit(solution)/shard_map/ppermute | solution.py:18
  184.6 88.8 %collective-permute-start.5 = (bf16[2,8,8,4,384]{4,3,2,1,0:T(4,128)(2,1)S(1)}, bf16[2,8,8,4,384]{4,3,2,1,0:T(4,128)(2,1)S(1)}, u32[]{:S(2)}, u32[]{:S(2)}) collective-permute-start(bf16[2,8,8,4,384]{4,3,2,1,0:T(4,128)(2,1)S(1)} %fusion.111), channel_id=1, source_target_pairs={{1,0},{0,1},{3,2},{2,3},{5,4},{4,5},{7,6},{6,7},{9,8},{8,9},{11,10... | collective-permute-start | bytes 1179656 | tf_op jit(solution)/shard_map/ppermute | solution.py:18
  (12 other events, 23.6 us)
Sparse Core Ops, SparseCore 0:
  131.1 137.4 all-reduce.2
where the time goes:
time: 284 us; the launch traced here: 282 us
  waiting for transfers between devices  118 us (42%)
  matrix products  83.3 us (29%)
  blocking collectives  37.9 us (13%)
  between operations  14.4 us (5%)
  other arithmetic  13 us (5%)
  starting transfers between devices  11.4 us (4%)
  local copies, waits for them, and re-layouts  3.69 us (1%)
    psum x1, waiting for transfers between devices, local(): summed = lax.psum((totals[0], totals[1], totals[2]), ('gx', 'gy', 'gz'))  82.3 us
    psum x1, blocking collectives, local(): summed = lax.psum((totals[0], totals[1], totals[2]), ('gx', 'gy', 'gz'))  37.9 us
    ppermute x6, waiting for transfers between devices, shifted_2(): return lax.ppermute(block, axis, route)  35.4 us
    dot_general x2, matrix products, group_pass(): jnp.einsum('hqk,khd->qhd', d_scores, key_rows, preferred_element_type=jnp...  23.2 us
    dot_general x2, matrix products, group_pass(): jnp.einsum('hqk,qhd->khd', d_scores, queries, preferred_element_type=jnp....  18.5 us
    ppermute x6, starting transfers between devices, shifted_2(): return lax.ppermute(block, axis, route)  11.4 us
    sub x2, matrix products, group_pass(): exp_terms = jnp.exp(scores - top_score)  9.57 us
    dot_general x2, matrix products, group_pass(): jnp.einsum('hqk,qhd->khd', probs_low, d_mixed, preferred_element_type=jnp...  9.15 us
  transfers between devices with their start and end apart: 7, of which 5 were waited for; matrix products, arithmetic and copies ran while one was open for 2% of the time, Pallas kernels for 0%

commit v1 on v0

v1 whole, which is shorter than its diff:
```python
import functools

import jax
import jax.numpy as jnp
from jax import lax
from jax.experimental import pallas as pl
from jax.experimental.pallas import tpu as pltpu
from jax.sharding import PartitionSpec as P

D = 384
HEADS = 12
HDIM = 32
WIN = 8
HALF = WIN // 2
OCT = HALF**3
ROWS = WIN**3
LANES = 128
PER_GROUP = LANES // HDIM
GROUPS = D // LANES
GRAD_ROWS = 4 * GROUPS * D
PARTS = 3
EPSILON = 1e-05
SCALE = HDIM ** (-0.5)
LOG2E = 1.4426950408889634
AXES = ("gx", "gy", "gz")
MESH = pl.DeviceIdType.MESH
VMEM_LIMIT = 56 * 1024 * 1024

OCTANTS = [(k // 4, k // 2 % 2, k % 2) for k in range(8)]


def neighbour(octant, direction):
    place = []
    for bit, axis in zip(octant, AXES, strict=True):
        size = lax.axis_size(axis)
        at = lax.axis_index(axis)
        place.append(at if bit else lax.rem(at + size + direction, size))
    return tuple(place)


def stages():
    found = []
    for axis in ("gy", "gz", "gx"):
        step = 1
        while step < lax.axis_size(axis):
            found.append((axis, step))
            step *= 2
    return found


def my_bit(axis, step):
    return lax.rem(lax.axis_index(axis) // step, 2)


def partner(axis, step):
    place = []
    for name in AXES:
        at = lax.axis_index(name)
        place.append(at + step * (1 - 2 * my_bit(axis, step)) if name == axis else at)
    return tuple(place)


def part_plan(order):
    plan, held = [], GRAD_ROWS // PARTS
    for axis, step in order:
        halved = held % 32 == 0
        if halved:
            held //= 2
        plan.append((axis, step, held, halved))
    return plan


def exchange_kernel(block_ref, window_ref, send_sem, recv_sem, own_sem):
    barrier = pltpu.get_barrier_semaphore()
    for octant in OCTANTS[:7]:
        pl.semaphore_signal(barrier, inc=1, device_id=neighbour(octant, 1), device_id_type=MESH)
    own = pltpu.make_async_copy(block_ref.at[7], window_ref.at[7], own_sem)
    own.start()
    pl.semaphore_wait(barrier, 7)
    copies = []
    for k, octant in enumerate(OCTANTS[:7]):
        copy = pltpu.make_async_remote_copy(
            src_ref=block_ref.at[k],
            dst_ref=window_ref.at[k],
            send_sem=send_sem.at[k],
            recv_sem=recv_sem.at[k],
            device_id=neighbour(octant, -1),
            device_id_type=MESH,
        )
        copy.start()
        copies.append(copy)
    own.wait()
    for copy in copies:
        copy.wait()


def dot(a, b):
    return lax.dot_general(a, b, (((1,), (0,)), ((), ())), preferred_element_type=jnp.float32)


def dot_nt(a, b):
    return lax.dot_general(a, b, (((1,), (1,)), ((), ())), preferred_element_type=jnp.float32)


def window_kernel(
    window_ref,
    w_qkv_ref,
    w_proj_ref,
    gain_ref,
    back_ref,
    grad_ref,
    gain_grad_ref,
    unit,
    inv_std,
    normed,
    qkv,
    d_mixed,
    d_qkv,
    mixed_t,
):
    rows = window_ref[:, :D].astype(jnp.float32)
    centred = rows - jnp.mean(rows, axis=-1, keepdims=True)
    inv = lax.rsqrt(jnp.mean(centred * centred, axis=-1, keepdims=True) + EPSILON)
    inv_std[...] = inv
    unit_rows = centred * inv
    unit[...] = unit_rows
    normed[...] = (unit_rows * gain_ref[...]).astype(jnp.bfloat16)
    qkv[...] = dot(normed[...], w_qkv_ref[...]).astype(jnp.bfloat16)
    d_mixed[...] = dot_nt(window_ref[:, D:], w_proj_ref[...]).astype(jnp.bfloat16)

    lane = lax.broadcasted_iota(jnp.int32, (ROWS, LANES), 1)

    def group(g, carry):
        at = [pl.ds(pl.multiple_of(part * D + g * LANES, LANES), LANES) for part in range(3)]
        queries, key_rows, values = (qkv[:, where] for where in at)
        cot = d_mixed[:, at[0]]
        keys_t = key_rows.T
        values_t = values.T
        d_keys = jnp.zeros((ROWS, LANES), jnp.float32)
        d_values = jnp.zeros((ROWS, LANES), jnp.float32)
        d_queries_t = []
        mixed_parts = []
        for h in range(PER_GROUP):
            mine = (lane >= h * HDIM) & (lane < (h + 1) * HDIM)
            own_queries = jnp.where(mine, queries, jnp.zeros_like(queries))
            own_cot = jnp.where(mine, cot, jnp.zeros_like(cot))
            head = slice(h * HDIM, (h + 1) * HDIM)
            scores = dot_nt(key_rows, own_queries)
            top = jnp.max(scores, axis=0, keepdims=True)
            exp_terms = jnp.exp2((scores - top) * (SCALE * LOG2E))
            probs = exp_terms * (1.0 / jnp.sum(exp_terms, axis=0, keepdims=True))
            probs_low = probs.astype(jnp.bfloat16)
            mixed_parts.append(dot(values_t[head], probs_low).astype(jnp.bfloat16))
            d_values += dot(probs_low, own_cot)
            d_probs = dot_nt(values, own_cot)
            total = jnp.sum(probs * d_probs, axis=0, keepdims=True)
            d_scores = (probs * (d_probs - total) * SCALE).astype(jnp.bfloat16)
            d_queries_t.append(dot(keys_t[head], d_scores).astype(jnp.bfloat16))
            d_keys += dot(d_scores, own_queries)
        mixed_t[at[0], :] = jnp.concatenate(mixed_parts, axis=0)
        d_qkv[:, at[0]] = jnp.concatenate(d_queries_t, axis=0).T
        d_qkv[:, at[1]] = d_keys.astype(jnp.bfloat16)
        d_qkv[:, at[2]] = d_values.astype(jnp.bfloat16)
        return carry

    lax.fori_loop(0, GROUPS, group, 0)

    back_ref[:, :D] = dot(mixed_t[...].T, w_proj_ref[...]).astype(jnp.bfloat16)
    normed_t = normed[...].T
    for j in range(3 * GROUPS):
        grad_ref[j * D : (j + 1) * D, :] = dot(normed_t, d_qkv[:, j * LANES : (j + 1) * LANES])
    for j in range(GROUPS):
        start = (3 * GROUPS + j) * D
        grad_ref[start : start + D, :] = dot(
            mixed_t[...], window_ref[:, D + j * LANES : D + (j + 1) * LANES]
        )
    d_normed = dot_nt(d_qkv[...], w_qkv_ref[...])
    unit_rows = unit[...]
    gain_term = jnp.sum(d_normed * unit_rows, axis=0, keepdims=True)
    gain_grad_ref[...] = jnp.zeros_like(gain_grad_ref)
    for j in range(GROUPS):
        gain_grad_ref[j : j + 1, :] = gain_term[:, j * LANES : (j + 1) * LANES]
    scaled = d_normed * gain_ref[...]
    back_ref[:, D:] = (
        inv_std[...]
        * (
            scaled
            - jnp.mean(scaled, axis=-1, keepdims=True)
            - unit_rows * jnp.mean(scaled * unit_rows, axis=-1, keepdims=True)
        )
    ).astype(jnp.bfloat16)


def return_kernel(
    order,
    back_ref,
    grad_ref,
    gain_ref,
    restored_ref,
    total_ref,
    gain_total_ref,
    acc,
    landing,
    gain_landing,
    back_send,
    back_recv,
    own_sem,
    reduce_send,
    reduce_recv,
    gather_send,
    gather_recv,
    gain_send,
    gain_recv,
):
    count = len(order)
    barrier = pltpu.get_barrier_semaphore()
    for octant in OCTANTS[:7]:
        pl.semaphore_signal(barrier, inc=1, device_id=neighbour(octant, -1), device_id_type=MESH)
    for axis, step in order:
        pl.semaphore_signal(barrier, inc=1, device_id=partner(axis, step), device_id_type=MESH)
    own = pltpu.make_async_copy(back_ref.at[7], restored_ref.at[7], own_sem)
    own.start()
    pl.semaphore_wait(barrier, 7 + count)

    plans = [part_plan(order[:1] + order[1 + p :] + order[1 : 1 + p]) for p in range(PARTS)]
    base = GRAD_ROWS // PARTS
    low = [jnp.int32(p * base) for p in range(PARTS)]
    pending = []

    def send_terms(p, s):
        axis, step, rows, halved = plans[p][s]
        bit = my_bit(axis, step)
        offset = p * landing.shape[0] // PARTS + sum(entry[2] for entry in plans[p][:s])
        start = low[p] + (1 - bit) * rows if halved else low[p]
        source = grad_ref if s == 0 else acc
        copy = pltpu.make_async_remote_copy(
            src_ref=source.at[pl.ds(pl.multiple_of(start, 16), rows)],
            dst_ref=landing.at[pl.ds(offset, rows)],
            send_sem=reduce_send.at[p, s],
            recv_sem=reduce_recv.at[p, s],
            device_id=partner(axis, step),
            device_id_type=MESH,
        )
        copy.start()
        keep = low[p] + bit * rows if halved else low[p]
        return copy, keep, offset, rows, halved

    def send_gain(s):
        axis, step = order[s]
        copy = pltpu.make_async_remote_copy(
            src_ref=gain_ref if s == 0 else gain_total_ref,
            dst_ref=gain_landing.at[s],
            send_sem=gain_send.at[s],
            recv_sem=gain_recv.at[s],
            device_id=partner(axis, step),
            device_id_type=MESH,
        )
        copy.start()
        return copy

    for s in range(count):
        started = [send_terms(p, s) for p in range(PARTS)]
        gain_copy = send_gain(s)
        if s == 0:
            backs = []
            for k, octant in enumerate(OCTANTS[:7]):
                copy = pltpu.make_async_remote_copy(
                    src_ref=back_ref.at[k],
                    dst_ref=restored_ref.at[k],
                    send_sem=back_send.at[k],
                    recv_sem=back_recv.at[k],
                    device_id=neighbour(octant, 1),
                    device_id_type=MESH,
                )
                copy.start()
                backs.append(copy)
        for p, (copy, keep, offset, rows, halved) in enumerate(started):
            source = grad_ref if s == 0 else acc
            copy.wait_recv()
            if halved:
                pending.append(copy)
            else:
                copy.wait_send()
            where = pl.ds(pl.multiple_of(keep, 16), rows)
            acc[where, :] = source[where, :] + landing[offset : offset + rows, :]
            low[p] = keep
        gain_copy.wait()
        previous = gain_ref if s == 0 else gain_total_ref
        gain_total_ref[...] = previous[...] + gain_landing[s]

    for p in range(PARTS):
        where = pl.ds(pl.multiple_of(low[p], 16), plans[p][-1][2])
        total_ref[where, :] = acc[where, :].astype(jnp.bfloat16)

    for s in reversed(range(count)):
        gathers = []
        for p in range(PARTS):
            axis, step, rows, halved = plans[p][s]
            if not halved:
                continue
            where = pl.ds(pl.multiple_of(low[p], 16), rows)
            copy = pltpu.make_async_remote_copy(
                src_ref=total_ref.at[where],
                dst_ref=total_ref.at[where],
                send_sem=gather_send.at[p, s],
                recv_sem=gather_recv.at[p, s],
                device_id=partner(axis, step),
                device_id_type=MESH,
            )
            copy.start()
            gathers.append(copy)
            low[p] = low[p] - my_bit(axis, step) * rows
        for copy in gathers:
            copy.wait_recv()
            pending.append(copy)

    for copy in pending:
        copy.wait_send()
    own.wait()
    for copy in backs:
        copy.wait()


def in_vmem(count):
    return [pl.BlockSpec(memory_space=pltpu.VMEM)] * count


def exchange(block):
    return pl.pallas_call(
        exchange_kernel,
        out_shape=jax.ShapeDtypeStruct(block.shape, block.dtype),
        in_specs=in_vmem(1),
        out_specs=in_vmem(1)[0],
        scratch_shapes=[
            pltpu.SemaphoreType.DMA((7,)),
            pltpu.SemaphoreType.DMA((7,)),
            pltpu.SemaphoreType.DMA,
        ],
        compiler_params=pltpu.CompilerParams(
            collective_id=0, has_side_effects=True, vmem_limit_bytes=VMEM_LIMIT
        ),
    )(block)


def window_pass(window, w_qkv, w_proj, norm_gain):
    low, wide = jnp.bfloat16, jnp.float32
    return pl.pallas_call(
        window_kernel,
        out_shape=(
            jax.ShapeDtypeStruct((ROWS, 2 * D), low),
            jax.ShapeDtypeStruct((GRAD_ROWS, LANES), wide),
            jax.ShapeDtypeStruct((8, LANES), wide),
        ),
        in_specs=in_vmem(4),
        out_specs=tuple(in_vmem(3)),
        scratch_shapes=[
            pltpu.VMEM((ROWS, D), wide),
            pltpu.VMEM((ROWS, 1), wide),
            pltpu.VMEM((ROWS, D), low),
            pltpu.VMEM((ROWS, 3 * D), low),
            pltpu.VMEM((ROWS, D), low),
            pltpu.VMEM((ROWS, 3 * D), low),
            pltpu.VMEM((D, ROWS), low),
        ],
        compiler_params=pltpu.CompilerParams(vmem_limit_bytes=VMEM_LIMIT),
    )(window, w_qkv, w_proj, norm_gain)


def send_back(back, grad, gain):
    order = stages()
    count = len(order)
    landing_rows = PARTS * sum(entry[2] for entry in part_plan(order))
    dma = pltpu.SemaphoreType.DMA
    return pl.pallas_call(
        functools.partial(return_kernel, order),
        out_shape=(
            jax.ShapeDtypeStruct(back.shape, back.dtype),
            jax.ShapeDtypeStruct(grad.shape, jnp.bfloat16),
            jax.ShapeDtypeStruct(gain.shape, gain.dtype),
        ),
        in_specs=in_vmem(3),
        out_specs=tuple(in_vmem(3)),
        scratch_shapes=[
            pltpu.VMEM(grad.shape, jnp.float32),
            pltpu.VMEM((landing_rows, LANES), jnp.float32),
            pltpu.VMEM((count, *gain.shape), jnp.float32),
            dma((7,)),
            dma((7,)),
            dma,
            dma((PARTS, count)),
            dma((PARTS, count)),
            dma((PARTS, count)),
            dma((PARTS, count)),
            dma((count,)),
            dma((count,)),
        ],
        compiler_params=pltpu.CompilerParams(
            collective_id=1, has_side_effects=True, vmem_limit_bytes=VMEM_LIMIT
        ),
    )(back, grad, gain)


def local(tokens, frozen, cotangent, w_qkv, w_proj, norm_gain):
    mask = frozen[..., None] == 1
    kept = jnp.where(mask, tokens, jnp.zeros_like(tokens))
    block = jnp.concatenate([kept, cotangent], axis=-1)
    block = block.reshape(2, HALF, 2, HALF, 2, HALF, 2 * D).transpose(0, 2, 4, 1, 3, 5, 6)
    window = exchange(block.reshape(8, OCT, 2 * D)).reshape(ROWS, 2 * D)
    back, grad, gain = window_pass(window, w_qkv, w_proj, norm_gain.reshape(1, D))
    restored, grad, gain = send_back(back.reshape(8, OCT, 2 * D), grad, gain)
    restored = restored.reshape(2, 2, 2, HALF, HALF, HALF, 2 * D).transpose(0, 3, 1, 4, 2, 5, 6)
    restored = restored.reshape(WIN, WIN, WIN, 2 * D).astype(jnp.float32)
    block_out = (kept.astype(jnp.float32) + restored[..., :D]).astype(jnp.bfloat16)
    tokens_grad = jnp.where(
        mask, cotangent.astype(jnp.float32) + restored[..., D:], jnp.zeros((), jnp.float32)
    ).astype(jnp.bfloat16)
    everyone = ROWS
    for axis in AXES:
        everyone *= lax.axis_size(axis)
    grad_scale = everyone ** (-0.5)
    grad = grad.reshape(4 * GROUPS, D, LANES).astype(jnp.float32) * grad_scale
    qkv_grad = grad[: 3 * GROUPS].transpose(1, 0, 2).reshape(D, 3 * D)
    proj_grad = grad[3 * GROUPS :].transpose(1, 0, 2).reshape(D, D)
    return (block_out, tokens_grad, qkv_grad, proj_grad, gain[:GROUPS].reshape(D) * grad_scale)


def solution(mesh):
    lattice = P(*AXES, None)
    return jax.shard_map(
        local,
        mesh=mesh,
        in_specs=(lattice, P(*AXES), lattice, P(), P(), P()),
        out_specs=(lattice, lattice, P(), P(), P()),
        check_vma=False,
    )
```

time: 284 us -> 112 us (0.39)
  waiting for transfers between devices: 118 us -> 0 us
  Pallas kernels: 0 us -> 91.6 us
  matrix products: 83.3 us -> 0 us
  blocking collectives: 37.9 us -> 0 us
  between operations: 14.4 us -> 0.74 us
  starting transfers between devices: 11.4 us -> 0 us
  local copies, waits for them, and re-layouts: 3.69 us -> 12.9 us
  other arithmetic: 13 us -> 6.58 us
    pallas_call x0 -> x3, Pallas kernels: none -> 91.6 us  [the longest x1 55.2 us: send_back(): pl.pallas_call(functools.partial(return_kernel, order), out_shape=(jax.Sh...]
    psum x1 -> x0, waiting for transfers between devices: 82.3 us -> none  [local(): summed = lax.psum((totals[0], totals[1], totals[2]), ('gx', 'gy', 'gz'))]
    dot_general x16 -> x0, matrix products: 73.8 us -> none  [the longest x2 23.2 us: group_pass(): jnp.einsum('hqk,khd->qhd', d_scores, key_rows, preferred_element_type=jnp...]
    psum x1 -> x0, blocking collectives: 37.9 us -> none  [local(): summed = lax.psum((totals[0], totals[1], totals[2]), ('gx', 'gy', 'gz'))]
    ppermute x6 -> x0, waiting for transfers between devices: 35.4 us -> none  [shifted_2(): return lax.ppermute(block, axis, route)]
    ppermute x6 -> x0, starting transfers between devices: 11.4 us -> none  [shifted_2(): return lax.ppermute(block, axis, route)]
    sub x2 -> x0, matrix products: 9.57 us -> none  [group_pass(): exp_terms = jnp.exp(scores - top_score)]
    mul x3 -> x2, other arithmetic: 5.29 us -> 1.41 us  [the longest x1 1.25 us: local(): gain[:GROUPS].reshape(D) * grad_scale]
  transfers between devices with their start and end apart: 7 -> 0, of which waited for: 5 -> 0; matrix products, arithmetic and copies ran while one was open for 2% -> 0% of each run, Pallas kernels for 0% -> 0%
where the time goes in v1:
time: 112 us
  Pallas kernels  91.6 us (82%)
  local copies, waits for them, and re-layouts  12.9 us (12%)
  other arithmetic  6.58 us (6%)
    pallas_call x1, Pallas kernels, send_back(): pl.pallas_call(functools.partial(return_kernel, order), out_shape=(jax.Sh...  55.2 us
    pallas_call x1, Pallas kernels, window_pass(): pl.pallas_call(window_kernel, out_shape=(jax.ShapeDtypeStruct((ROWS, 2 *...  20.7 us
    pallas_call x1, Pallas kernels, exchange(): pl.pallas_call(exchange_kernel, out_shape=jax.ShapeDtypeStruct(block.shap...  15.8 us
    unnamed x8, local copies, waits for them, and re-layouts  3.93 us
    slice x2, local copies, waits for them, and re-layouts, local(): qkv_grad = grad[:3 * GROUPS].transpose(1, 0, 2).reshape(D, 3 * D)  3.61 us
    convert_element_type x3, local copies, waits for them, and re-layouts, local(): restored = restored.reshape(WIN, WIN, WIN, 2 * D).astype(jnp.float32)  2.34 us

profile of v1, /device:TPU:1, one launch (start us, length us, event | category | flops | bytes accessed | tf_op | source)
XLA Modules:
  0.0 111.9 jit_solution(18026464226557345397)
XLA Ops:
  0.6 1.2 %reshape.51.gain_ref = f32[1,384]{1,0:T(1,128)} reshape(f32[384]{0:T(512)} %param.11) | data formatting | bytes 3072 | tf_op jit(solution)/shard_map/reshape | solution.py:409
  1.9 0.8 broadcast_compare_fusion
  2.6 1.1 %broadcast_select_fusion = bf16[8,8,8,384]{3,2,1,0:T(8,128)(2,1)S(1)} fusion(bf16[8,8,8,384]{3,2,1,0:T(8,128)(2,1)} %param.6, pred[8,8,8]{2,1,0:T(8,128)(4,1)S(1)} %broadcast_compare_fusion), kind=kLoop, calls=%fused_computation.8 | loop fusion | flops 196608 | bytes 786944 | tf_op jit(solution)/shard_map/jit(_where)/select_n | solution.py:405
  3.8 1.1 pad_maximum_fusion
  4.8 0.2 reshape.48
  5.0 0.3 copy.22
  5.4 1.1 reshape.49.block_ref
  6.4 15.8 %shard_map.101 = bf16[8,64,768]{2,1,0:T(8,128)(2,1)} custom-call(bf16[8,64,768]{2,1,0:T(8,128)(2,1)} %reshape.49.block_ref), custom_call_target="tpu_custom_call" | custom-call | tf_op jit(solution)/shard_map/pallas_call | solution.py:329
  22.2 20.7 %shard_map.102 = (bf16[512,768]{1,0:T(8,128)(2,1)}, f32[4608,128]{1,0:T(8,128)}, f32[8,128]{1,0:T(8,128)}) custom-call(bf16[512,768]{1,0:T(8,128)(2,1)} %bitcast.23, bf16[384,1152]{1,0:T(8,128)(2,1)} %w_qkv_ref.1, bf16[384,384]{1,0:T(8,128)(2,1)} %w_proj_ref.1, f32[1,384]{1,0:T(1,128)} %reshape.51.gain_ref), custom_call_target="tpu_custom_call" | custom-call | tf_op jit(solution)/shard_map/pallas_call | solution.py:347
  42.9 55.2 %shard_map.103 = (bf16[8,64,768]{2,1,0:T(8,128)(2,1)}, bf16[4608,128]{1,0:T(8,128)(2,1)}, f32[8,128]{1,0:T(8,128)}) custom-call(bf16[8,64,768]{2,1,0:T(8,128)(2,1)} %bitcast.25, f32[4608,128]{1,0:T(8,128)} %get-tuple-element.12.grad_ref, f32[8,128]{1,0:T(8,128)} %get-tuple-element.13.gain_ref), custom_call_target="tpu_custom_call" | custom-call | tf_op jit(solution)/shard_map/pallas_call | solution.py:374
  98.1 1.3 %multiply_bitcast_fusion = f32[384]{0:T(512)} fusion(f32[8,128]{1,0:T(8,128)} %get-tuple-element.16), kind=kLoop, calls=%fused_computation.10 | loop fusion | flops 384 | bytes 3072 | tf_op jit(solution)/shard_map/mul | solution.py:424
  99.3 1.7 %reshape.56 = f32[2,2,2,4,4,4,768]{6,5,4,3,2,1,0:T(4,128)S(1)} reshape(bf16[8,64,768]{2,1,0:T(8,128)(2,1)} %get-tuple-element.14) | data formatting | bytes 2359296 | tf_op jit(solution)/shard_map/convert_element_type | solution.py:412
  101.0 0.1 copy.16
  101.1 0.0 copy-start.1
  101.2 0.5 reshape.55
  101.7 0.4 copy-done.1
  102.1 2.2 %fusion.1 = (bf16[8,8,8,384]{3,2,1,0:T(8,128)(2,1)}, bf16[8,8,8,384]{3,2,1,0:T(8,128)(2,1)}) fusion(f32[8,8,8,768]{3,2,1,0:T(8,128)S(1)} %reshape.55, bf16[8,8,8,384]{3,2,1,0:T(8,128)(2,1)S(1)} %copy-done.1, pred[8,8,8]{2,1,0:T(8,128)(4,1)S(1)} %broadcast_compare_fusion, bf16[8,8,8,384]{3,2,1,0:T(8,128)(2,1)} %param.6), kind=kLoop, calls=%fused_computation.3 | loop fusion | flops 1572864 | bytes 3146240 | tf_op jit(solution)/shard_map/convert_element_type | solution.py:416
  104.4 0.2 convert_multiply_fusion
  104.5 1.4 %slice.30 = f32[3456,128]{1,0:T(8,128)} slice(f32[4608,128]{1,0:T(8,128)S(1)} %convert_multiply_fusion), slice={[0:3456], [0:128]} | slice | bytes 3538944 | tf_op jit(solution)/shard_map/slice | solution.py:422
  106.0 0.5 copy-done
  106.5 2.2 %copy.17 = f32[9,384,128]{1,2,0:T(8,128)S(1)} copy(f32[9,384,128]{2,1,0:T(8,128)} %bitcast.19) | data formatting | bytes 3538944 | tf_op jit(solution)/shard_map/slice | solution.py:422
  108.7 1.9 %copy.19 = f32[384,1152]{1,0:T(8,128)} copy(f32[384,1152]{0,1:T(8,128)S(1)} %bitcast.20) | data formatting | bytes 3538944
  110.6 0.2 copy.18
  110.8 1.1 copy.20
  (5 shorter events, 0.0 us)
Async XLA Ops:
  101.1 1.0 copy-start.1
  102.1 2.2 %copy-start.2 = (bf16[4608,128]{1,0:T(8,128)(2,1)S(1)}, bf16[4608,128]{1,0:T(8,128)(2,1)}, u32[]{:S(2)}) copy-start(bf16[4608,128]{1,0:T(8,128)(2,1)} %get-tuple-element.15) | copy-start | bytes 3538948
  104.5 2.0 %copy-start = (f32[4608,128]{1,0:T(8,128)}, f32[4608,128]{1,0:T(8,128)S(1)}, u32[]{:S(2)}) copy-start(f32[4608,128]{1,0:T(8,128)S(1)} %convert_multiply_fusion) | copy-start | bytes 7077892
  108.7 1.9 %slice-start = ((f32[4608,128]{1,0:T(8,128)}), f32[1152,128]{1,0:T(8,128)S(1)}, s32[]{:S(2)}) async-start(f32[4608,128]{1,0:T(8,128)} %copy-done), calls=%async_computation | async-start | bytes 1179648 | tf_op jit(solution)/shard_map/slice | solution.py:423

commit v2 on v1

v2 whole, which is shorter than its diff:
```python
import functools

import jax
import jax.numpy as jnp
from jax import lax
from jax.experimental import pallas as pl
from jax.experimental.pallas import tpu as pltpu
from jax.sharding import PartitionSpec as P

D = 384
HEADS = 12
HDIM = 32
WIN = 8
HALF = WIN // 2
OCT = HALF**3
ROWS = WIN**3
LANES = 128
PER_GROUP = LANES // HDIM
GROUPS = D // LANES
GRAD_ROWS = 4 * GROUPS * D
PARTS = 3
EPSILON = 1e-05
SCALE = HDIM ** (-0.5)
LOG2E = 1.4426950408889634
AXES = ("gx", "gy", "gz")
MESH = pl.DeviceIdType.MESH
VMEM_LIMIT = 56 * 1024 * 1024

OCTANTS = [
    (1, 1, 1),
    (1, 1, 0),
    (1, 0, 1),
    (0, 1, 1),
    (1, 0, 0),
    (0, 1, 0),
    (0, 0, 1),
    (0, 0, 0),
]


def neighbour(octant, direction):
    place = []
    for bit, axis in zip(octant, AXES, strict=True):
        size = lax.axis_size(axis)
        at = lax.axis_index(axis)
        place.append(at if bit else lax.rem(at + size + direction, size))
    return tuple(place)


def stages():
    bits = []
    for axis in ("gy", "gz", "gx"):
        step = 1
        while step < lax.axis_size(axis):
            bits.append((axis, step))
            step *= 2
    return [bits[:1]] + [bits[i : i + 2] for i in range(1, len(bits), 2)]


def my_bit(axis, step):
    return lax.rem(lax.axis_index(axis) // step, 2)


def partner(bits, flips):
    place = {axis: lax.axis_index(axis) for axis in AXES}
    digit = 0
    for i, (axis, step) in enumerate(bits):
        bit = my_bit(axis, step)
        if flips >> i & 1:
            place[axis] = place[axis] + step * (1 - 2 * bit)
            bit = 1 - bit
        digit = digit + bit * 2**i
    return tuple(place[axis] for axis in AXES), digit


def plan_stages(order):
    plan, held = [], GRAD_ROWS // PARTS
    for bits in order:
        count = 2 ** len(bits)
        divided = held % (16 * count) == 0
        if divided:
            held //= count
        plan.append((bits, held, divided))
    return plan


def tree_sum(terms):
    while len(terms) > 1:
        terms = [a + b for a, b in zip(terms[::2], terms[1::2], strict=True)]
    return terms[0]


def remote(src, dst, send_sem, recv_sem, device):
    copy = pltpu.make_async_remote_copy(
        src_ref=src,
        dst_ref=dst,
        send_sem=send_sem,
        recv_sem=recv_sem,
        device_id=device,
        device_id_type=MESH,
    )
    copy.start()
    return copy


def reduce_part(plan, p, grad, landing, total_ref, sems, unsent):
    reduce_send, reduce_recv, gather_send, gather_recv = sems
    low = p * (GRAD_ROWS // PARTS)
    offset = p * (landing.shape[0] // PARTS)
    for s, (bits, rows, divided) in enumerate(plan):
        copies = []
        for flips in range(1, 2 ** len(bits)):
            device, digit = partner(bits, flips)
            start = pl.multiple_of(low + digit * rows, 16) if divided else low
            copies.append(
                remote(
                    grad.at[pl.ds(start, rows)],
                    landing.at[pl.ds(offset + (flips - 1) * rows, rows)],
                    reduce_send.at[p, s, flips - 1],
                    reduce_recv.at[p, s, flips - 1],
                    device,
                )
            )
        yield
        for copy in copies:
            copy.wait_recv()
            if divided:
                unsent.append(copy)
            else:
                copy.wait_send()
        if divided:
            low = pl.multiple_of(low + partner(bits, 0)[1] * rows, 16)
        where = pl.ds(low, rows)
        terms = [grad[where, :]]
        for _ in copies:
            terms.append(landing[offset : offset + rows, :])
            offset += rows
        grad[where, :] = tree_sum(terms)
    where = pl.ds(low, plan[-1][1])
    total_ref[where, :] = grad[where, :].astype(jnp.bfloat16)
    for s, (bits, rows, divided) in reversed(list(enumerate(plan))):
        if not divided:
            continue
        copies = []
        where = pl.ds(low, rows)
        for flips in range(1, 2 ** len(bits)):
            copies.append(
                remote(
                    total_ref.at[where],
                    total_ref.at[where],
                    gather_send.at[p, s, flips - 1],
                    gather_recv.at[p, s, flips - 1],
                    partner(bits, flips)[0],
                )
            )
        yield
        for copy in copies:
            copy.wait_recv()
            unsent.append(copy)
        low = pl.multiple_of(low - partner(bits, 0)[1] * rows, 16)


def reduce_gain(order, gain_ref, landing, send_sem, recv_sem):
    for s, bits in enumerate(order):
        copies = []
        for flips in range(1, 2 ** len(bits)):
            copies.append(
                remote(
                    gain_ref,
                    landing.at[s, flips - 1],
                    send_sem.at[s, flips - 1],
                    recv_sem.at[s, flips - 1],
                    partner(bits, flips)[0],
                )
            )
        yield
        for copy in copies:
            copy.wait()
        terms = [gain_ref[...]] + [landing[s, i] for i in range(len(copies))]
        gain_ref[...] = tree_sum(terms)


def dot(a, b):
    return lax.dot_general(a, b, (((1,), (0,)), ((), ())), preferred_element_type=jnp.float32)


def dot_nt(a, b):
    return lax.dot_general(a, b, (((1,), (1,)), ((), ())), preferred_element_type=jnp.float32)


def split_octants(block):
    pairs = block.reshape(HALF, 2, WIN, WIN, D)
    even, odd = pairs[:, 0], pairs[:, 1]
    first = lax.broadcasted_iota(jnp.int32, even.shape, 2) < HALF
    halves = [
        jnp.where(first, even, swapped(odd)),
        jnp.where(first, swapped(even), odd),
    ]
    found = []
    for ox, oy, oz in OCTANTS:
        part = halves[oz][2 * ox : 2 * ox + 2, HALF * oy : HALF * oy + HALF]
        found.append(part.reshape(OCT, D))
    return found


def join_octants(octants):
    parts = dict(zip(OCTANTS, octants, strict=True))
    halves = []
    for oz in range(2):
        rows = []
        for ox in range(2):
            both = [parts[ox, oy, oz].reshape(2, HALF, WIN, D) for oy in range(2)]
            rows.append(jnp.concatenate(both, axis=1))
        halves.append(jnp.concatenate(rows, axis=0))
    lower, upper = halves
    first = lax.broadcasted_iota(jnp.int32, lower.shape, 2) < HALF
    even = jnp.where(first, lower, swapped(upper))
    odd = jnp.where(first, swapped(lower), upper)
    return jnp.stack([even, odd], axis=1).reshape(WIN, WIN, WIN, D)


def swapped(rows):
    shape = rows.shape
    return pltpu.roll(rows.reshape(-1, WIN, D), HALF, 1).reshape(shape)


def kept_tokens(tokens_ref, frozen_ref):
    mask = jnp.broadcast_to(frozen_ref[...], (WIN, WIN, WIN, D)) == 1
    return mask, jnp.where(mask, tokens_ref[...].astype(jnp.float32), 0.0)


def main_kernel(
    order,
    tokens_ref,
    frozen_ref,
    cot_ref,
    w_qkv_ref,
    w_proj_ref,
    gain_ref,
    restored_ref,
    total_ref,
    gain_total_ref,
    block,
    window,
    unit,
    inv_std,
    normed,
    qkv,
    d_mixed,
    d_qkv,
    mixed_t,
    back,
    grad,
    landing,
    gain_landing,
    out_send,
    out_recv,
    back_send,
    back_recv,
    reduce_send,
    reduce_recv,
    gather_send,
    gather_recv,
    gain_send,
    gain_recv,
):
    barrier = pltpu.get_barrier_semaphore()
    greeted = 0
    for octant in OCTANTS[1:]:
        for direction in (-1, 1):
            device = neighbour(octant, direction)
            pl.semaphore_signal(barrier, inc=1, device_id=device, device_id_type=MESH)
            greeted += 1
    for bits in order:
        for flips in range(1, 2 ** len(bits)):
            device = partner(bits, flips)[0]
            pl.semaphore_signal(barrier, inc=1, device_id=device, device_id_type=MESH)
            greeted += 1

    kept = split_octants(kept_tokens(tokens_ref, frozen_ref)[1])
    cot = split_octants(cot_ref[...].astype(jnp.float32))
    for k in range(8):
        target = block.at[k] if k else window.at[0:OCT]
        target[:, :D] = kept[k].astype(jnp.bfloat16)
        target[:, D:] = cot[k].astype(jnp.bfloat16)
    pl.semaphore_wait(barrier, greeted)
    unsent = []
    arriving = [None]
    for k in range(1, 8):
        device = neighbour(OCTANTS[k], -1)
        where = pl.ds(k * OCT, OCT)
        arriving.append(
            remote(block.at[k], window.at[where], out_send.at[k - 1], out_recv.at[k - 1], device)
        )

    half_rows = ROWS // 2
    for part in range(2):
        for copy in arriving[4 * part : 4 * part + 4]:
            if copy is not None:
                copy.wait_recv()
                unsent.append(copy)
        at = slice(part * half_rows, (part + 1) * half_rows)
        rows = window[at, :D].astype(jnp.float32)
        centred = rows - jnp.mean(rows, axis=-1, keepdims=True)
        inv = lax.rsqrt(jnp.mean(centred * centred, axis=-1, keepdims=True) + EPSILON)
        inv_std[at, :] = inv
        unit_part = centred * inv
        unit[at, :] = unit_part
        normed_part = (unit_part * gain_ref[...]).astype(jnp.bfloat16)
        normed[at, :] = normed_part
        qkv[at, :] = dot(normed_part, w_qkv_ref[...]).astype(jnp.bfloat16)
        d_mixed[at, :] = dot_nt(window[at, D:], w_proj_ref[...]).astype(jnp.bfloat16)

    plan = plan_stages(order)
    sems = (reduce_send, reduce_recv, gather_send, gather_recv)
    running = []

    def advance():
        for task in list(running):
            if next(task, "done") == "done":
                running.remove(task)

    def launch(task):
        next(task)
        running.append(task)

    lane = lax.broadcasted_iota(jnp.int32, (ROWS, LANES), 1)
    normed_t = normed[...].T
    window_cot = window[:, D:]

    for g in range(GROUPS):
        at = [slice(part * D + g * LANES, part * D + (g + 1) * LANES) for part in range(3)]
        queries, key_rows, values = (qkv[:, where] for where in at)
        cot_rows = d_mixed[:, at[0]]
        keys_t = key_rows.T
        values_t = values.T
        d_keys = jnp.zeros((ROWS, LANES), jnp.float32)
        d_values = jnp.zeros((ROWS, LANES), jnp.float32)
        d_queries_t = []
        mixed_parts = []
        for h in range(PER_GROUP):
            mine = (lane >= h * HDIM) & (lane < (h + 1) * HDIM)
            own_queries = jnp.where(mine, queries, jnp.zeros_like(queries))
            own_cot = jnp.where(mine, cot_rows, jnp.zeros_like(cot_rows))
            head = slice(h * HDIM, (h + 1) * HDIM)
            scores = dot_nt(key_rows, own_queries)
            top = jnp.max(scores, axis=0, keepdims=True)
            exp_terms = jnp.exp2((scores - top) * (SCALE * LOG2E))
            probs = exp_terms * (1.0 / jnp.sum(exp_terms, axis=0, keepdims=True))
            probs_low = probs.astype(jnp.bfloat16)
            mixed_parts.append(dot(values_t[head], probs_low).astype(jnp.bfloat16))
            d_values += dot(probs_low, own_cot)
            d_probs = dot_nt(values, own_cot)
            total = jnp.sum(probs * d_probs, axis=0, keepdims=True)
            d_scores = (probs * (d_probs - total) * SCALE).astype(jnp.bfloat16)
            d_queries_t.append(dot(keys_t[head], d_scores).astype(jnp.bfloat16))
            d_keys += dot(d_scores, own_queries)
        mixed_t[at[0], :] = jnp.concatenate(mixed_parts, axis=0)
        d_qkv[:, at[0]] = jnp.concatenate(d_queries_t, axis=0).T
        d_qkv[:, at[1]] = d_keys.astype(jnp.bfloat16)
        d_qkv[:, at[2]] = d_values.astype(jnp.bfloat16)
        start = g * (GRAD_ROWS // PARTS)
        for part in range(3):
            grad[start : start + D, :] = dot(normed_t, d_qkv[:, at[part]])
            start += D
        proj_term = dot(mixed_t[at[0], :], window_cot)
        for j in range(GROUPS):
            grad[start : start + LANES, :] = proj_term[:, j * LANES : (j + 1) * LANES]
            start += LANES
        advance()
        launch(reduce_part(plan, g, grad, landing, total_ref, sems, unsent))

    def send_back(which):
        for k in range(1, 8):
            copy = remote(
                back.at[which, k],
                restored_ref.at[which, k],
                back_send.at[which, k - 1],
                back_recv.at[which, k - 1],
                neighbour(OCTANTS[k], 1),
            )
            unsent.append(copy)
            returning.append(copy)

    returning = []
    branch = dot(mixed_t[...].T, w_proj_ref[...]).astype(jnp.bfloat16)
    back[0] = branch.reshape(8, OCT, D)
    send_back(0)
    advance()
    d_normed = dot_nt(d_qkv[...], w_qkv_ref[...])
    unit_rows = unit[...]
    gain_term = jnp.sum(d_normed * unit_rows, axis=0, keepdims=True)
    gain_total_ref[...] = jnp.zeros_like(gain_total_ref)
    for j in range(GROUPS):
        gain_total_ref[j : j + 1, :] = gain_term[:, j * LANES : (j + 1) * LANES]
    launch(reduce_gain(order, gain_total_ref, gain_landing, gain_send, gain_recv))
    scaled = d_normed * gain_ref[...]
    d_rows = (
        inv_std[...]
        * (
            scaled
            - jnp.mean(scaled, axis=-1, keepdims=True)
            - unit_rows * jnp.mean(scaled * unit_rows, axis=-1, keepdims=True)
        )
    ).astype(jnp.bfloat16)
    back[1] = d_rows.reshape(8, OCT, D)
    send_back(1)
    for which in range(2):
        restored_ref[which, 0] = back[which, 0]
    while running:
        advance()
    for copy in returning:
        copy.wait_recv()
    for copy in unsent:
        copy.wait_send()


def finish_kernel(
    scale,
    tokens_ref,
    frozen_ref,
    cot_ref,
    restored_ref,
    total_ref,
    gain_total_ref,
    out_ref,
    tokens_grad_ref,
    qkv_grad_ref,
    proj_grad_ref,
    gain_grad_ref,
):
    wide = jnp.float32
    mask, kept = kept_tokens(tokens_ref, frozen_ref)
    branch = join_octants([restored_ref[0, k].astype(wide) for k in range(8)])
    out_ref[...] = (kept + branch).astype(jnp.bfloat16)
    d_rows = join_octants([restored_ref[1, k].astype(wide) for k in range(8)])
    both = cot_ref[...].astype(wide) + d_rows
    tokens_grad_ref[...] = jnp.where(mask, both, 0.0).astype(jnp.bfloat16)
    start = 0
    for g in range(GROUPS):
        for part in range(3):
            column = part * D + g * LANES
            qkv_grad_ref[:, column : column + LANES] = total_ref[start : start + D, :].astype(wide) * scale
            start += D
        for j in range(GROUPS):
            proj_grad_ref[g * LANES : (g + 1) * LANES, j * LANES : (j + 1) * LANES] = (
                total_ref[start : start + LANES, :].astype(wide) * scale
            )
            start += LANES
    gain_grad_ref[...] = gain_total_ref[...] * scale


def in_vmem(count):
    return [pl.BlockSpec(memory_space=pltpu.VMEM)] * count


def local(tokens, frozen, cotangent, w_qkv, w_proj, norm_gain):
    low, wide = jnp.bfloat16, jnp.float32
    shape = jax.ShapeDtypeStruct
    frozen = frozen[..., None]
    order = stages()
    count = len(order)
    landing_rows = PARTS * sum(
        (2 ** len(bits) - 1) * rows for bits, rows, _ in plan_stages(order)
    )
    dma = pltpu.SemaphoreType.DMA
    restored, total, gain = pl.pallas_call(
        functools.partial(main_kernel, order),
        out_shape=(
            shape((2, 8, OCT, D), low),
            shape((GRAD_ROWS, LANES), low),
            shape((8, LANES), wide),
        ),
        in_specs=in_vmem(6),
        out_specs=tuple(in_vmem(3)),
        scratch_shapes=[
            pltpu.VMEM((8, OCT, 2 * D), low),
            pltpu.VMEM((ROWS, 2 * D), low),
            pltpu.VMEM((ROWS, D), wide),
            pltpu.VMEM((ROWS, 1), wide),
            pltpu.VMEM((ROWS, D), low),
            pltpu.VMEM((ROWS, 3 * D), low),
            pltpu.VMEM((ROWS, D), low),
            pltpu.VMEM((ROWS, 3 * D), low),
            pltpu.VMEM((D, ROWS), low),
            pltpu.VMEM((2, 8, OCT, D), low),
            pltpu.VMEM((GRAD_ROWS, LANES), wide),
            pltpu.VMEM((landing_rows, LANES), wide),
            pltpu.VMEM((count, 3, 8, LANES), wide),
            dma((7,)),
            dma((7,)),
            dma((2, 7)),
            dma((2, 7)),
            dma((PARTS, count, 3)),
            dma((PARTS, count, 3)),
            dma((PARTS, count, 3)),
            dma((PARTS, count, 3)),
            dma((count, 3)),
            dma((count, 3)),
        ],
        compiler_params=pltpu.CompilerParams(
            collective_id=0, has_side_effects=True, vmem_limit_bytes=VMEM_LIMIT
        ),
    )(tokens, frozen, cotangent, w_qkv, w_proj, norm_gain.reshape(1, D))
    everyone = ROWS
    for axis in AXES:
        everyone *= lax.axis_size(axis)
    block_out, tokens_grad, qkv_grad, proj_grad, gain = pl.pallas_call(
        functools.partial(finish_kernel, everyone ** (-0.5)),
        out_shape=(
            shape(tokens.shape, low),
            shape(tokens.shape, low),
            shape((D, 3 * D), wide),
            shape((D, D), wide),
            shape((8, LANES), wide),
        ),
        in_specs=in_vmem(6),
        out_specs=tuple(in_vmem(5)),
        compiler_params=pltpu.CompilerParams(vmem_limit_bytes=VMEM_LIMIT),
    )(tokens, frozen, cotangent, restored, total, gain)
    return (block_out, tokens_grad, qkv_grad, proj_grad, gain[:GROUPS].reshape(D))


def solution(mesh):
    lattice = P(*AXES, None)
    return jax.shard_map(
        local,
        mesh=mesh,
        in_specs=(lattice, P(*AXES), lattice, P(), P(), P()),
        out_specs=(lattice, lattice, P(), P(), P()),
        check_vma=False,
    )
```

time: 112 us -> 79.6 us (0.71)
  Pallas kernels: 91.6 us -> 74.2 us
  local copies, waits for them, and re-layouts: 12.9 us -> 4.4 us
  other arithmetic: 6.58 us -> 0 us
    pallas_call x3 -> x2, Pallas kernels: 91.6 us -> 74.2 us  [the longest x1 70.3 us: local(): pl.pallas_call(functools.partial(main_kernel, order), out_shape=(shape((2...]
    unnamed x8 -> x0, local copies, waits for them, and re-layouts: 3.93 us -> none
    slice x5 -> x0, local copies, waits for them, and re-layouts: 3.84 us -> none  [the longest x2 3.61 us: local(): qkv_grad = grad[:3 * GROUPS].transpose(1, 0, 2).reshape(D, 3 * D)]
    convert_element_type x3 -> x0, local copies, waits for them, and re-layouts: 2.34 us -> none  [local(): restored = restored.reshape(WIN, WIN, WIN, 2 * D).astype(jnp.float32)]
    convert_element_type x1 -> x0, other arithmetic: 2.22 us -> none  [local(): tokens_grad = jnp.where(mask, cotangent.astype(jnp.float32) + restored[.....]
    broadcast_in_dim x0 -> x1, local copies, waits for them, and re-layouts: none -> 1.9 us  [local(): frozen = frozen[..., None]]
    mul x2 -> x0, other arithmetic: 1.41 us -> none  [the longest x1 1.25 us: local(): gain[:GROUPS].reshape(D) * grad_scale]
    select_n x1 -> x0, other arithmetic: 1.13 us -> none  [local(): kept = jnp.where(mask, tokens, jnp.zeros_like(tokens))]
where the time goes in v2:
time: 79.6 us; the launch traced here: 79.2 us
  Pallas kernels  74.2 us (93%)
  local copies, waits for them, and re-layouts  4.4 us (6%)
    pallas_call x1, Pallas kernels, local(): pl.pallas_call(functools.partial(main_kernel, order), out_shape=(shape((2...  70.3 us
    pallas_call x1, Pallas kernels, local(): pl.pallas_call(functools.partial(finish_kernel, everyone ** (-0.5)), out_...  3.92 us
    broadcast_in_dim x1, local copies, waits for them, and re-layouts, local(): frozen = frozen[..., None]  1.9 us

profile of v2, /device:TPU:1, one launch (start us, length us, event | category | flops | bytes accessed | tf_op | source)
XLA Modules:
  0.0 79.2 jit_solution(17069532849840283845)
XLA Ops:
  0.6 1.2 %reshape.16.gain_ref = f32[1,384]{1,0:T(1,128)} reshape(f32[384]{0:T(512)} %param.11) | data formatting | bytes 3072 | tf_op jit(solution)/shard_map/reshape | solution.py:504
  1.9 1.9 %copy.12.frozen_ref = s32[8,8,8,1]{3,2,1,0:T(8,128)} copy(s32[8,8,8,1]{2,1,0,3:T(8,128)} %bitcast.3) | data formatting | bytes 4096 | tf_op jit(solution)/shard_map/broadcast_in_dim | solution.py:460
  3.8 70.3 %shard_map.101 = (bf16[2,8,64,384]{3,2,1,0:T(8,128)(2,1)}, bf16[4608,128]{1,0:T(8,128)(2,1)}, f32[8,128]{1,0:T(8,128)}) custom-call(bf16[8,8,8,384]{3,2,1,0:T(8,128)(2,1)} %tokens_ref.3, s32[8,8,8,1]{3,2,1,0:T(8,128)} %copy.12.frozen_ref, bf16[8,8,8,384]{3,2,1,0:T(8,128)(2,1)} %cot_ref.3, bf16[384,1152]{1,0:T(8,128)(2,1)} %w_qkv_ref.1, ...), custom_call_target="tpu_custom_call" | custom-call | tf_op jit(solution)/shard_map/pallas_call | solution.py:467
  74.1 3.9 %shard_map.102 = (bf16[8,8,8,384]{3,2,1,0:T(8,128)(2,1)}, bf16[8,8,8,384]{3,2,1,0:T(8,128)(2,1)}, f32[384,1152]{1,0:T(8,128)}, f32[384,384]{1,0:T(8,128)}, f32[8,128]{1,0:T(8,128)}) custom-call(bf16[8,8,8,384]{3,2,1,0:T(8,128)(2,1)} %tokens_ref.3, s32[8,8,8,1]{3,2,1,0:T(8,128)} %copy.12.frozen_ref, bf16[8,8,8,384]{3,2,1,0:T(8,128)(2,1)} %cot_ref.3, ...), custom_call_target="tpu_custom_call" | custom-call | tf_op jit(solution)/shard_map/pallas_call | solution.py:508
  78.0 1.3 %slice_bitcast_fusion = f32[384]{0:T(512)} fusion(f32[8,128]{1,0:T(8,128)} %get-tuple-element.20), kind=kLoop, calls=%fused_computation | loop fusion | bytes 3072 | tf_op jit(solution)/shard_map/reshape | solution.py:521

commit v3 on v2

--- a/solution.py
+++ b/solution.py
@@ -225,7 +225,7 @@
 
 
 def kept_tokens(tokens_ref, frozen_ref):
-    mask = jnp.broadcast_to(frozen_ref[...], (WIN, WIN, WIN, D)) == 1
+    mask = jnp.broadcast_to(frozen_ref[...][..., None], (WIN, WIN, WIN, D)) == 1
     return mask, jnp.where(mask, tokens_ref[...].astype(jnp.float32), 0.0)
 
 
@@ -293,6 +293,7 @@
             remote(block.at[k], window.at[where], out_send.at[k - 1], out_recv.at[k - 1], device)
         )
 
+    norm_gain = gain_ref[...].reshape(1, D)
     half_rows = ROWS // 2
     for part in range(2):
         for copy in arriving[4 * part : 4 * part + 4]:
@@ -306,27 +307,29 @@
         inv_std[at, :] = inv
         unit_part = centred * inv
         unit[at, :] = unit_part
-        normed_part = (unit_part * gain_ref[...]).astype(jnp.bfloat16)
+        normed_part = (unit_part * norm_gain).astype(jnp.bfloat16)
         normed[at, :] = normed_part
         qkv[at, :] = dot(normed_part, w_qkv_ref[...]).astype(jnp.bfloat16)
         d_mixed[at, :] = dot_nt(window[at, D:], w_proj_ref[...]).astype(jnp.bfloat16)
 
     plan = plan_stages(order)
     sems = (reduce_send, reduce_recv, gather_send, gather_recv)
-    running = []
-
-    def advance():
-        for task in list(running):
-            if next(task, "done") == "done":
-                running.remove(task)
-
-    def launch(task):
+    tasks = {}
+
+    def launch(name, task):
+        tasks[name] = task
         next(task)
-        running.append(task)
+
+    def advance(*names):
+        for name in names:
+            if name in tasks and next(tasks[name], "done") == "done":
+                del tasks[name]
 
     lane = lax.broadcasted_iota(jnp.int32, (ROWS, LANES), 1)
     normed_t = normed[...].T
     window_cot = window[:, D:]
+
+    polls = {(1, 1): (0,), (2, 1): (1,), (2, 2): (0,)}
 
     for g in range(GROUPS):
         at = [slice(part * D + g * LANES, part * D + (g + 1) * LANES) for part in range(3)]
@@ -355,6 +358,7 @@
             d_scores = (probs * (d_probs - total) * SCALE).astype(jnp.bfloat16)
             d_queries_t.append(dot(keys_t[head], d_scores).astype(jnp.bfloat16))
             d_keys += dot(d_scores, own_queries)
+            advance(*polls.get((g, h), ()))
         mixed_t[at[0], :] = jnp.concatenate(mixed_parts, axis=0)
         d_qkv[:, at[0]] = jnp.concatenate(d_queries_t, axis=0).T
         d_qkv[:, at[1]] = d_keys.astype(jnp.bfloat16)
@@ -367,8 +371,7 @@
         for j in range(GROUPS):
             grad[start : start + LANES, :] = proj_term[:, j * LANES : (j + 1) * LANES]
             start += LANES
-        advance()
-        launch(reduce_part(plan, g, grad, landing, total_ref, sems, unsent))
+        launch(g, reduce_part(plan, g, grad, landing, total_ref, sems, unsent))
 
     def send_back(which):
         for k in range(1, 8):
@@ -385,16 +388,16 @@
     returning = []
     branch = dot(mixed_t[...].T, w_proj_ref[...]).astype(jnp.bfloat16)
     back[0] = branch.reshape(8, OCT, D)
+    d_normed = dot_nt(d_qkv[...], w_qkv_ref[...])
+    advance(2, 0)
     send_back(0)
-    advance()
-    d_normed = dot_nt(d_qkv[...], w_qkv_ref[...])
     unit_rows = unit[...]
     gain_term = jnp.sum(d_normed * unit_rows, axis=0, keepdims=True)
     gain_total_ref[...] = jnp.zeros_like(gain_total_ref)
     for j in range(GROUPS):
         gain_total_ref[j : j + 1, :] = gain_term[:, j * LANES : (j + 1) * LANES]
-    launch(reduce_gain(order, gain_total_ref, gain_landing, gain_send, gain_recv))
-    scaled = d_normed * gain_ref[...]
+    launch(GROUPS, reduce_gain(order, gain_total_ref, gain_landing, gain_send, gain_recv))
+    scaled = d_normed * norm_gain
     d_rows = (
         inv_std[...]
         * (
@@ -407,8 +410,9 @@
     send_back(1)
     for which in range(2):
         restored_ref[which, 0] = back[which, 0]
-    while running:
-        advance()
+    advance(1, 0, 1, 3, 2, 0, 1, 2, 3, 1, 2)
+    while tasks:
+        advance(*tasks)
     for copy in returning:
         copy.wait_recv()
     for copy in unsent:
@@ -447,7 +451,9 @@
                 total_ref[start : start + LANES, :].astype(wide) * scale
             )
             start += LANES
-    gain_grad_ref[...] = gain_total_ref[...] * scale
+    for j in range(GROUPS):
+        row = gain_total_ref[j : j + 1, :] * scale
+        gain_grad_ref[j * LANES : (j + 1) * LANES] = row.reshape(LANES)
 
 
 def in_vmem(count):
@@ -457,7 +463,6 @@
 def local(tokens, frozen, cotangent, w_qkv, w_proj, norm_gain):
     low, wide = jnp.bfloat16, jnp.float32
     shape = jax.ShapeDtypeStruct
-    frozen = frozen[..., None]
     order = stages()
     count = len(order)
     landing_rows = PARTS * sum(
@@ -501,24 +506,23 @@
         compiler_params=pltpu.CompilerParams(
             collective_id=0, has_side_effects=True, vmem_limit_bytes=VMEM_LIMIT
         ),
-    )(tokens, frozen, cotangent, w_qkv, w_proj, norm_gain.reshape(1, D))
+    )(tokens, frozen, cotangent, w_qkv, w_proj, norm_gain)
     everyone = ROWS
     for axis in AXES:
         everyone *= lax.axis_size(axis)
-    block_out, tokens_grad, qkv_grad, proj_grad, gain = pl.pallas_call(
+    return pl.pallas_call(
         functools.partial(finish_kernel, everyone ** (-0.5)),
         out_shape=(
             shape(tokens.shape, low),
             shape(tokens.shape, low),
             shape((D, 3 * D), wide),
             shape((D, D), wide),
-            shape((8, LANES), wide),
+            shape((D,), wide),
         ),
         in_specs=in_vmem(6),
         out_specs=tuple(in_vmem(5)),
         compiler_params=pltpu.CompilerParams(vmem_limit_bytes=VMEM_LIMIT),
     )(tokens, frozen, cotangent, restored, total, gain)
-    return (block_out, tokens_grad, qkv_grad, proj_grad, gain[:GROUPS].reshape(D))
 
 
 def solution(mesh):

time: 79.6 us -> 74.8 us (0.940)
  local copies, waits for them, and re-layouts: 4.4 us -> 0 us
    reshape x2 -> x0, local copies, waits for them, and re-layouts: 2.5 us -> none  [the longest x1 1.25 us: local(): gain[:GROUPS].reshape(D)]
    broadcast_in_dim x1 -> x0, local copies, waits for them, and re-layouts: 1.9 us -> none  [local(): frozen = frozen[..., None]]
where the time goes in v3:
time: 74.8 us; the launch traced here: 74.7 us
  Pallas kernels  74 us (99%)
    pallas_call x1, Pallas kernels, local(): pl.pallas_call(functools.partial(main_kernel, order), out_shape=(shape((2...  70.2 us
    pallas_call x1, Pallas kernels, local(): pl.pallas_call(functools.partial(finish_kernel, everyone ** (-0.5)), out_...  3.85 us

profile of v3, /device:TPU:1, one launch (start us, length us, event | category | flops | bytes accessed | tf_op | source)
XLA Modules:
  0.0 74.7 jit_solution(14750976748050233012)
XLA Ops:
  0.6 70.2 %shard_map.101 = (bf16[2,8,64,384]{3,2,1,0:T(8,128)(2,1)}, bf16[4608,128]{1,0:T(8,128)(2,1)}, f32[8,128]{1,0:T(8,128)}) custom-call(bf16[8,8,8,384]{3,2,1,0:T(8,128)(2,1)} %tokens_ref.3, s32[8,8,8]{2,1,0:T(8,128)} %frozen_ref.3, bf16[8,8,8,384]{3,2,1,0:T(8,128)(2,1)} %cot_ref.3, bf16[384,1152]{1,0:T(8,128)(2,1)} %w_qkv_ref.1, bf16[384,384]{1,0:T(8,128)(2,1)} %w_proj_ref.1, ...), custom_call_target="tpu_custom_call" | custom-call | tf_op jit(solution)/shard_map/pallas_call | solution.py:472
  70.8 3.9 %shard_map.102 = (bf16[8,8,8,384]{3,2,1,0:T(8,128)(2,1)}, bf16[8,8,8,384]{3,2,1,0:T(8,128)(2,1)}, f32[384,1152]{1,0:T(8,128)}, f32[384,384]{1,0:T(8,128)}, f32[384]{0:T(512)}) custom-call(bf16[8,8,8,384]{3,2,1,0:T(8,128)(2,1)} %tokens_ref.3, s32[8,8,8]{2,1,0:T(8,128)} %frozen_ref.3, bf16[8,8,8,384]{3,2,1,0:T(8,128)(2,1)} %cot_ref.3, ...), custom_call_target="tpu_custom_call" | custom-call | tf_op jit(solution)/shard_map/pallas_call | solution.py:513

commit v4 on v3

--- a/solution.py
+++ b/solution.py
@@ -249,6 +249,7 @@
     d_mixed,
     d_qkv,
     mixed_t,
+    probs,
     back,
     grad,
     landing,
@@ -329,49 +330,30 @@
     normed_t = normed[...].T
     window_cot = window[:, D:]
 
-    polls = {(1, 1): (0,), (2, 1): (1,), (2, 2): (0,)}
+    def columns(part, g):
+        return slice(part * D + g * LANES, part * D + (g + 1) * LANES)
+
+    def own_lanes(rows, h):
+        mine = (lane >= h * HDIM) & (lane < (h + 1) * HDIM)
+        return jnp.where(mine, rows, jnp.zeros_like(rows))
 
     for g in range(GROUPS):
-        at = [slice(part * D + g * LANES, part * D + (g + 1) * LANES) for part in range(3)]
-        queries, key_rows, values = (qkv[:, where] for where in at)
-        cot_rows = d_mixed[:, at[0]]
-        keys_t = key_rows.T
+        queries, key_rows, values = (qkv[:, columns(part, g)] for part in range(3))
         values_t = values.T
-        d_keys = jnp.zeros((ROWS, LANES), jnp.float32)
-        d_values = jnp.zeros((ROWS, LANES), jnp.float32)
-        d_queries_t = []
         mixed_parts = []
         for h in range(PER_GROUP):
-            mine = (lane >= h * HDIM) & (lane < (h + 1) * HDIM)
-            own_queries = jnp.where(mine, queries, jnp.zeros_like(queries))
-            own_cot = jnp.where(mine, cot_rows, jnp.zeros_like(cot_rows))
-            head = slice(h * HDIM, (h + 1) * HDIM)
-            scores = dot_nt(key_rows, own_queries)
+            scores = dot_nt(key_rows, own_lanes(queries, h))
             top = jnp.max(scores, axis=0, keepdims=True)
             exp_terms = jnp.exp2((scores - top) * (SCALE * LOG2E))
-            probs = exp_terms * (1.0 / jnp.sum(exp_terms, axis=0, keepdims=True))
-            probs_low = probs.astype(jnp.bfloat16)
-            mixed_parts.append(dot(values_t[head], probs_low).astype(jnp.bfloat16))
-            d_values += dot(probs_low, own_cot)
-            d_probs = dot_nt(values, own_cot)
-            total = jnp.sum(probs * d_probs, axis=0, keepdims=True)
-            d_scores = (probs * (d_probs - total) * SCALE).astype(jnp.bfloat16)
-            d_queries_t.append(dot(keys_t[head], d_scores).astype(jnp.bfloat16))
-            d_keys += dot(d_scores, own_queries)
-            advance(*polls.get((g, h), ()))
-        mixed_t[at[0], :] = jnp.concatenate(mixed_parts, axis=0)
-        d_qkv[:, at[0]] = jnp.concatenate(d_queries_t, axis=0).T
-        d_qkv[:, at[1]] = d_keys.astype(jnp.bfloat16)
-        d_qkv[:, at[2]] = d_values.astype(jnp.bfloat16)
-        start = g * (GRAD_ROWS // PARTS)
-        for part in range(3):
-            grad[start : start + D, :] = dot(normed_t, d_qkv[:, at[part]])
-            start += D
-        proj_term = dot(mixed_t[at[0], :], window_cot)
-        for j in range(GROUPS):
-            grad[start : start + LANES, :] = proj_term[:, j * LANES : (j + 1) * LANES]
-            start += LANES
-        launch(g, reduce_part(plan, g, grad, landing, total_ref, sems, unsent))
+            head_probs = exp_terms * (1.0 / jnp.sum(exp_terms, axis=0, keepdims=True))
+            probs[g * PER_GROUP + h] = head_probs
+            head = slice(h * HDIM, (h + 1) * HDIM)
+            mixed_parts.append(
+                dot(values_t[head], head_probs.astype(jnp.bfloat16)).astype(jnp.bfloat16)
+            )
+        mixed_t[columns(0, g), :] = jnp.concatenate(mixed_parts, axis=0)
+
+    returning = []
 
     def send_back(which):
         for k in range(1, 8):
@@ -385,12 +367,46 @@
             unsent.append(copy)
             returning.append(copy)
 
-    returning = []
     branch = dot(mixed_t[...].T, w_proj_ref[...]).astype(jnp.bfloat16)
     back[0] = branch.reshape(8, OCT, D)
+    send_back(0)
+
+    polls = {(1, 2): (0,), (2, 2): (1,)}
+
+    for g in range(GROUPS):
+        queries, key_rows, values = (qkv[:, columns(part, g)] for part in range(3))
+        cot_rows = d_mixed[:, columns(0, g)]
+        keys_t = key_rows.T
+        d_keys = jnp.zeros((ROWS, LANES), jnp.float32)
+        d_values = jnp.zeros((ROWS, LANES), jnp.float32)
+        d_queries_t = []
+        for h in range(PER_GROUP):
+            own_queries = own_lanes(queries, h)
+            own_cot = own_lanes(cot_rows, h)
+            head = slice(h * HDIM, (h + 1) * HDIM)
+            head_probs = probs[g * PER_GROUP + h]
+            d_values += dot(head_probs.astype(jnp.bfloat16), own_cot)
+            d_probs = dot_nt(values, own_cot)
+            total = jnp.sum(head_probs * d_probs, axis=0, keepdims=True)
+            d_scores = (head_probs * (d_probs - total) * SCALE).astype(jnp.bfloat16)
+            d_queries_t.append(dot(keys_t[head], d_scores).astype(jnp.bfloat16))
+            d_keys += dot(d_scores, own_queries)
+            advance(*polls.get((g, h), ()))
+        d_qkv[:, columns(0, g)] = jnp.concatenate(d_queries_t, axis=0).T
+        d_qkv[:, columns(1, g)] = d_keys.astype(jnp.bfloat16)
+        d_qkv[:, columns(2, g)] = d_values.astype(jnp.bfloat16)
+        start = g * (GRAD_ROWS // PARTS)
+        for part in range(3):
+            grad[start : start + D, :] = dot(normed_t, d_qkv[:, columns(part, g)])
+            start += D
+        proj_term = dot(mixed_t[columns(0, g), :], window_cot)
+        for j in range(GROUPS):
+            grad[start : start + LANES, :] = proj_term[:, j * LANES : (j + 1) * LANES]
+            start += LANES
+        launch(g, reduce_part(plan, g, grad, landing, total_ref, sems, unsent))
+
     d_normed = dot_nt(d_qkv[...], w_qkv_ref[...])
-    advance(2, 0)
-    send_back(0)
+    advance(2)
     unit_rows = unit[...]
     gain_term = jnp.sum(d_normed * unit_rows, axis=0, keepdims=True)
     gain_total_ref[...] = jnp.zeros_like(gain_total_ref)
@@ -410,7 +426,7 @@
     send_back(1)
     for which in range(2):
         restored_ref[which, 0] = back[which, 0]
-    advance(1, 0, 1, 3, 2, 0, 1, 2, 3, 1, 2)
+    advance(0, 1, 3, 0, 2, 1, 3, 0, 2, 1, 0, 2, 1, 3, 2)
     while tasks:
         advance(*tasks)
     for copy in returning:
@@ -488,6 +504,7 @@
             pltpu.VMEM((ROWS, D), low),
             pltpu.VMEM((ROWS, 3 * D), low),
             pltpu.VMEM((D, ROWS), low),
+            pltpu.VMEM((HEADS, ROWS, ROWS), wide),
             pltpu.VMEM((2, 8, OCT, D), low),
             pltpu.VMEM((GRAD_ROWS, LANES), wide),
             pltpu.VMEM((landing_rows, LANES), wide),

time: 74.8 us -> 71 us (0.949)
  Pallas kernels: 74 us -> 70.2 us
    pallas_call x1, Pallas kernels: 70.2 us -> 66.4 us  [local(): pl.pallas_call(functools.partial(main_kernel, order), out_shape=(shape((2...]
where the time goes in v4:
time: 71 us; the launch traced here: 70.8 us
  Pallas kernels  70.2 us (99%)
    pallas_call x1, Pallas kernels, local(): pl.pallas_call(functools.partial(main_kernel, order), out_shape=(shape((2...  66.4 us
    pallas_call x1, Pallas kernels, local(): pl.pallas_call(functools.partial(finish_kernel, everyone ** (-0.5)), out_...  3.85 us

profile of v4, /device:TPU:1, one launch (start us, length us, event | category | flops | bytes accessed | tf_op | source)
XLA Modules:
  0.0 70.8 jit_solution(6044776097997423405)
XLA Ops:
  0.6 66.4 %shard_map.101 = (bf16[2,8,64,384]{3,2,1,0:T(8,128)(2,1)}, bf16[4608,128]{1,0:T(8,128)(2,1)}, f32[8,128]{1,0:T(8,128)}) custom-call(bf16[8,8,8,384]{3,2,1,0:T(8,128)(2,1)} %tokens_ref.3, s32[8,8,8]{2,1,0:T(8,128)} %frozen_ref.3, bf16[8,8,8,384]{3,2,1,0:T(8,128)(2,1)} %cot_ref.3, bf16[384,1152]{1,0:T(8,128)(2,1)} %w_qkv_ref.1, bf16[384,384]{1,0:T(8,128)(2,1)} %w_proj_ref.1, ...), custom_call_target="tpu_custom_call" | custom-call | tf_op jit(solution)/shard_map/pallas_call | solution.py:488
  67.0 3.9 %shard_map.102 = (bf16[8,8,8,384]{3,2,1,0:T(8,128)(2,1)}, bf16[8,8,8,384]{3,2,1,0:T(8,128)(2,1)}, f32[384,1152]{1,0:T(8,128)}, f32[384,384]{1,0:T(8,128)}, f32[384]{0:T(512)}) custom-call(bf16[8,8,8,384]{3,2,1,0:T(8,128)(2,1)} %tokens_ref.3, s32[8,8,8]{2,1,0:T(8,128)} %frozen_ref.3, bf16[8,8,8,384]{3,2,1,0:T(8,128)(2,1)} %cot_ref.3, ...), custom_call_target="tpu_custom_call" | custom-call | tf_op jit(solution)/shard_map/pallas_call | solution.py:530
